TPU v7x, 128 devices: a whole 4x4x4 slice. The times are simulated.
128 devices in a mesh: lat: 8 (over x_hi, y), lon: 16 (over z, x_lo, core).
Axes of the slice: x: 4 (x_hi: 2, x_lo: 2; x = x_hi * 2 + x_lo), y: 4, z: 4, core: 2. Of those that a mesh axis runs over, the one named last changes fastest.
Arguments:
- latent: bfloat16 [2, 192, 768, 512], P(None, 'lat', 'lon'), may hold values from -6 to 6
- cotangent: bfloat16 [2, 192, 768, 512], P(None, 'lat', 'lon'), may hold values from -6 to 6
- qkv_weight: bfloat16 [512, 1536], P(('lat', 'lon')), may hold values from -2 to 2
- out_weight: bfloat16 [512, 512], P(('lat', 'lon')), may hold values from -0.25 to 0.25
Outputs:
- output: bfloat16 [2, 192, 768, 512], P(None, 'lat', 'lon')
- grad_latent: bfloat16 [2, 192, 768, 512], P(None, 'lat', 'lon')
- grad_qkv: float32 [512, 1536], P(('lat', 'lon'))
- grad_out_weight: float32 [512, 512], P(('lat', 'lon'))
All inputs are finite; a program needn't handle non-finite values.
Results may differ from a plain program's by a relative error of at most 0.013.
Values may be sent and summed in bfloat16 or wider, within the bound.
A program may use at most 128 MiB of HBM per device.

v0:
```python
import math

import jax
import jax.numpy as jnp
from jax import lax
from jax.sharding import PartitionSpec as P

C = 512
HEADS = 8
HD = 64
WIN_LAT = 6
WIN_LON = 12


def passed_along(block, axis, distance):
    devices = range(lax.axis_size(axis))
    route = [((i - distance) % len(devices), i) for i in devices]
    return lax.ppermute(block, axis, route)


def product(pattern, left, right):
    return jnp.einsum(pattern, left, right, preferred_element_type=jnp.float32)


def matmul(left, right):
    return jnp.dot(left, right, preferred_element_type=jnp.float32)


def times_transposed(left, right):
    return lax.dot_general(
        left, right, (((1,), (1,)), ((), ())), preferred_element_type=jnp.float32
    )


def transposed_times(left, right):
    return lax.dot_general(
        left, right, (((0,), (0,)), ((), ())), preferred_element_type=jnp.float32
    )


def windowed(grid_block):
    levels, row_count, columns, features = grid_block.shape
    pieces = grid_block.reshape(levels, row_count, columns // WIN_LON, WIN_LON, features)
    return pieces.transpose(2, 0, 1, 3, 4).reshape(
        columns // WIN_LON, levels * row_count * WIN_LON, features
    )


def unwindowed(window_tiles, levels, row_count):
    window_count, tokens, features = window_tiles.shape
    pieces = window_tiles.reshape(window_count, levels, row_count, WIN_LON, features)
    return pieces.transpose(1, 2, 0, 3, 4).reshape(
        levels, row_count, window_count * WIN_LON, features
    )


def to_slabs(grid_block):
    levels, row_count, columns, features = grid_block.shape
    pieces = grid_block.reshape(levels, row_count // WIN_LAT, WIN_LAT, columns, features)
    return pieces.transpose(1, 0, 2, 3, 4)


def from_slabs(stacked):
    slab_count, levels, row_count, columns, features = stacked.shape
    return stacked.transpose(1, 0, 2, 3, 4).reshape(
        levels, slab_count * row_count, columns, features
    )


def slab_step(qkv_weight, out_weight, inputs):
    rolled_slab, cot_slab, flag_row = inputs
    levels, row_count, columns, features = rolled_slab.shape
    score_scale = HD ** (-0.5)
    tiles = windowed(rolled_slab)
    window_count, tokens = (tiles.shape[0], tiles.shape[1])
    widened = tiles.reshape(-1, C).astype(jnp.float32)
    centred = widened - jnp.mean(widened, -1, keepdims=True)
    inv_scale = lax.rsqrt(jnp.mean(centred * centred, -1, keepdims=True) + 1e-05)
    standard = centred * inv_scale
    normed = standard.astype(jnp.bfloat16)
    projections = matmul(normed, qkv_weight).astype(jnp.bfloat16)
    queries = projections[:, :C].reshape(window_count, tokens, HEADS, HD)
    key_heads = projections[:, C : 2 * C].reshape(window_count, tokens, HEADS, HD)
    values = projections[:, 2 * C :].reshape(window_count, tokens, HEADS, HD)
    flag_full = jnp.broadcast_to(flag_row[None, :, None, None], (levels, row_count, columns, 1))
    flag_tiles = windowed(flag_full)[:, :, 0]
    allowed = flag_tiles[:, None, :, None] == flag_tiles[:, None, None, :]
    scores = product("wqhd,wkhd->whqk", queries, key_heads) * score_scale
    scores = jnp.where(allowed, scores, -1e30)
    maximum = jnp.max(scores, -1, keepdims=True)
    shifted_exp = jnp.exp(scores - maximum)
    attention = shifted_exp / jnp.sum(shifted_exp, -1, keepdims=True)
    attention_low = attention.astype(jnp.bfloat16)
    context = product("whqk,wkhd->wqhd", attention_low, values).astype(jnp.bfloat16).reshape(-1, C)
    result = (widened + matmul(context, out_weight)).astype(jnp.bfloat16)
    incoming = windowed(cot_slab).reshape(-1, C)
    grad_context = times_transposed(incoming, out_weight).astype(jnp.bfloat16)
    out_term = transposed_times(context, incoming)
    context_heads = grad_context.reshape(window_count, tokens, HEADS, HD)
    grad_attention = product("wqhd,wkhd->whqk", context_heads, values)
    grad_values = product("whqk,wqhd->wkhd", attention_low, context_heads).astype(jnp.bfloat16)
    inner = jnp.sum(grad_attention * attention, -1, keepdims=True)
    grad_scores = (attention * (grad_attention - inner) * score_scale).astype(jnp.bfloat16)
    grad_queries = product("whqk,wkhd->wqhd", grad_scores, key_heads).astype(jnp.bfloat16)
    grad_keys = product("whqk,wqhd->wkhd", grad_scores, queries).astype(jnp.bfloat16)
    grad_packed = jnp.concatenate(
        [grad_queries.reshape(-1, C), grad_keys.reshape(-1, C), grad_values.reshape(-1, C)], 1
    )
    qkv_term = transposed_times(normed, grad_packed)
    grad_normed = times_transposed(grad_packed, qkv_weight)
    first_mean = jnp.mean(grad_normed, -1, keepdims=True)
    second_mean = jnp.mean(grad_normed * standard, -1, keepdims=True)
    grad_input = inv_scale * (grad_normed - first_mean - standard * second_mean) + incoming.astype(
        jnp.float32
    )
    grad_input = grad_input.astype(jnp.bfloat16)
    result_grid = unwindowed(result.reshape(window_count, tokens, C), levels, row_count)
    grad_grid = unwindowed(grad_input.reshape(window_count, tokens, C), levels, row_count)
    return (result_grid, grad_grid, qkv_term, out_term)


def run_layer(rolled, rolled_cot, row_flags, qkv_weight, out_weight):
    row_count = rolled.shape[1]
    flag_rows = row_flags.reshape(row_count // WIN_LAT, WIN_LAT)

    def advance(totals, inputs):
        result, grad_input, qkv_term, out_term = slab_step(qkv_weight, out_weight, inputs)
        return ((totals[0] + qkv_term, totals[1] + out_term), (result, grad_input))

    initial = (jnp.zeros((C, 3 * C), jnp.float32), jnp.zeros((C, C), jnp.float32))
    totals, outputs = lax.scan(
        advance, initial, (to_slabs(rolled), to_slabs(rolled_cot), flag_rows)
    )
    return (from_slabs(outputs[0]), from_slabs(outputs[1]), totals[0], totals[1])


def body(latent, cotangent, qkv_weight, out_weight):
    qkv_full, out_full = (
        lax.all_gather(qkv_weight, ("lat", "lon"), axis=0, tiled=True),
        lax.all_gather(out_weight, ("lat", "lon"), axis=0, tiled=True),
    )
    half_rows = WIN_LAT // 2
    half_cols = WIN_LON // 2
    rows_dev = latent.shape[1]
    cols_dev = latent.shape[2]
    lat_count = lax.axis_size("lat")
    lon_count = lax.axis_size("lon")
    strip_rows = jnp.stack([latent[:, :half_rows], cotangent[:, :half_rows]])
    arrived_rows = passed_along(strip_rows, "lat", -1)
    latent_rows = jnp.concatenate([latent[:, half_rows:], arrived_rows[0]], 1)
    cot_rows = jnp.concatenate([cotangent[:, half_rows:], arrived_rows[1]], 1)
    strip_cols = jnp.stack([latent_rows[:, :, :half_cols], cot_rows[:, :, :half_cols]])
    arrived_cols = passed_along(strip_cols, "lon", -1)
    rolled = jnp.concatenate([latent_rows[:, :, half_cols:], arrived_cols[0]], 2)
    rolled_cot = jnp.concatenate([cot_rows[:, :, half_cols:], arrived_cols[1]], 2)
    row_index = lax.axis_index("lat") * rows_dev + jnp.arange(rows_dev, dtype=jnp.int32) + half_rows
    row_flags = row_index % (rows_dev * lat_count) < half_rows
    result, grad_input, qkv_term, out_term = run_layer(
        rolled, rolled_cot, row_flags, qkv_full, out_full
    )
    back_cols = jnp.stack(
        [result[:, :, cols_dev - half_cols :], grad_input[:, :, cols_dev - half_cols :]]
    )
    returned_cols = passed_along(back_cols, "lon", 1)
    result_cols = jnp.concatenate([returned_cols[0], result[:, :, : cols_dev - half_cols]], 2)
    grad_cols = jnp.concatenate([returned_cols[1], grad_input[:, :, : cols_dev - half_cols]], 2)
    back_rows = jnp.stack(
        [result_cols[:, rows_dev - half_rows :], grad_cols[:, rows_dev - half_rows :]]
    )
    returned_rows = passed_along(back_rows, "lat", 1)
    output = jnp.concatenate([returned_rows[0], result_cols[:, : rows_dev - half_rows]], 1)
    grad_latent = jnp.concatenate([returned_rows[1], grad_cols[:, : rows_dev - half_rows]], 1)
    sum_qkv, sum_out = (
        lax.psum_scatter(qkv_term, ("lat", "lon"), scatter_dimension=0, tiled=True),
        lax.psum_scatter(out_term, ("lat", "lon"), scatter_dimension=0, tiled=True),
    )
    total_tokens = latent.shape[0] * rows_dev * cols_dev * lat_count * lon_count
    factor = 1.0 / math.sqrt(total_tokens)
    return (output, grad_latent, sum_qkv * factor, sum_out * factor)


def solution(mesh):
    in_specs = (
        P(None, "lat", "lon", None),
        P(None, "lat", "lon", None),
        P(("lat", "lon"), None),
        P(("lat", "lon"), None),
    )
    out_specs = (
        P(None, "lat", "lon", None),
        P(None, "lat", "lon", None),
        P(("lat", "lon"), None),
        P(("lat", "lon"), None),
    )
    return jax.shard_map(body, mesh=mesh, in_specs=in_specs, out_specs=out_specs, check_vma=False)
```

profile of v0, /device:TPU:1, one launch (start us, length us, event | category | flops | bytes accessed | tf_op | source)
XLA Modules:
  0.0 761.4 jit_solution(18345042137386535582)
XLA Ops:
  9.1 6.1 collective-permute-start
  16.7 2.9 copy.230
  20.8 6.7 collective-permute-done
  29.9 181.3 %all-gather.1 = bf16[128,4,512]{2,1,0:T(4,128)(2,1)S(1)} all-gather(bf16[1,4,512]{2,1,0:T(4,128)(2,1)S(1)} %bitcast.188), channel_id=1, replica_groups=mesh['lat'=8,'lon'=16] {'lat','lon'}, dimensions={0}, use_global_device_ids=true | all-gather | bytes 528384 | tf_op jit(solution)/shard_map/all_gather | solution.py:140
  218.8 4.4 maximum_bitcast_fusion.1
  223.2 4.9 maximum_bitcast_fusion
  228.1 3.7 reshape.136
  231.8 362.1 %while.17 = (s32[]{:T(128)}, f32[512,1536]{1,0:T(8,128)}, f32[512,512]{1,0:T(8,128)}, bf16[4,2,6,48,512]{4,3,2,0,1:T(8,128)(2,1)}, bf16[4,2,6,48,512]{4,3,2,0,1:...) while((s32[]{:T(128)}, f32[512,1536]{1,0:T(8,128)}, ...), condition=%wide.region_8.9_spmd.clone, body=%wide.region_0.8_spmd.clone.sunk | while | flops 4161186816 | bytes 125110976 | solution.py:131
  254.3 2.5 convolution_convert_fusion.6
  267.0 5.6 fusion.138
  272.6 2.8 fusion.142
  283.5 3.3 fusion.141
  288.3 4.6 fusion.137
  292.9 9.5 %fusion.140 = bf16[4,144,8,64]{1,3,2,0:T(8,128)(2,1)} fusion(bf16[4,144,8,64]{1,3,2,0:T(8,128)(2,1)} %copy.267, f32[4,8,144,144]{2,3,1,0:T(8,128)} %fusion.137, f32[4,8,144,144]{2,3,1,0:T(8,128)} %get-tuple-element.216, f32[4,8,144]{2,1,0:T(8,128)S(1)} %get-tuple-element.217), kind=kOutput, calls=%fused_computation.23.clone.1 | convolution fusion | flops 89879184 | bytes 6506496 | tf_op jit(solution)/shard_map/while/body/eval_jaxpr/whqk,wqhd->wkhd/dot_general | solution.py:22
  302.4 9.1 %fusion.139 = bf16[4,144,8,64]{1,3,2,0:T(8,128)(2,1)} fusion(bf16[4,144,8,64]{1,3,2,0:T(8,128)(2,1)S(1)} %copy-done.5, f32[4,8,144,144]{2,3,1,0:T(8,128)} %fusion.137, f32[4,8,144,144]{2,3,1,0:T(8,128)} %get-tuple-element.216, f32[4,8,144]{2,1,0:T(8,128)S(1)} %get-tuple-element.217), kind=kOutput, calls=%fused_computation.24.clone.1 | convolution fusion | flops 89879184 | bytes 6506496 | tf_op jit(solution)/shard_map/while/body/eval_jaxpr/whqk,wkhd->wqhd/dot_general | solution.py:22
  323.3 3.4 convolution_add_fusion.5
  339.5 2.5 convolution_convert_fusion.6
  352.1 5.7 fusion.138
  357.8 2.8 fusion.142
  367.1 2.8 convolution_add_fusion.6
  369.9 3.3 fusion.141
  374.7 4.6 fusion.137
  379.2 9.5 %fusion.140 = bf16[4,144,8,64]{1,3,2,0:T(8,128)(2,1)} fusion(bf16[4,144,8,64]{1,3,2,0:T(8,128)(2,1)} %copy.267, f32[4,8,144,144]{2,3,1,0:T(8,128)} %fusion.137, f32[4,8,144,144]{2,3,1,0:T(8,128)} %get-tuple-element.216, f32[4,8,144]{2,1,0:T(8,128)S(1)} %get-tuple-element.217), kind=kOutput, calls=%fused_computation.23.clone.1 | convolution fusion | flops 89879184 | bytes 6506496 | tf_op jit(solution)/shard_map/while/body/eval_jaxpr/whqk,wqhd->wkhd/dot_general | solution.py:22
  388.7 9.1 %fusion.139 = bf16[4,144,8,64]{1,3,2,0:T(8,128)(2,1)} fusion(bf16[4,144,8,64]{1,3,2,0:T(8,128)(2,1)S(1)} %copy-done.5, f32[4,8,144,144]{2,3,1,0:T(8,128)} %fusion.137, f32[4,8,144,144]{2,3,1,0:T(8,128)} %get-tuple-element.216, f32[4,8,144]{2,1,0:T(8,128)S(1)} %get-tuple-element.217), kind=kOutput, calls=%fused_computation.24.clone.1 | convolution fusion | flops 89879184 | bytes 6506496 | tf_op jit(solution)/shard_map/while/body/eval_jaxpr/whqk,wkhd->wqhd/dot_general | solution.py:22
  409.7 5.3 convolution_add_fusion.5
  427.7 2.5 convolution_convert_fusion.6
  440.3 5.7 fusion.138
  446.0 2.8 fusion.142
  455.4 2.8 convolution_add_fusion.6
  458.1 3.3 fusion.141
  462.9 4.6 fusion.137
  467.5 9.5 %fusion.140 = bf16[4,144,8,64]{1,3,2,0:T(8,128)(2,1)} fusion(bf16[4,144,8,64]{1,3,2,0:T(8,128)(2,1)} %copy.267, f32[4,8,144,144]{2,3,1,0:T(8,128)} %fusion.137, f32[4,8,144,144]{2,3,1,0:T(8,128)} %get-tuple-element.216, f32[4,8,144]{2,1,0:T(8,128)S(1)} %get-tuple-element.217), kind=kOutput, calls=%fused_computation.23.clone.1 | convolution fusion | flops 89879184 | bytes 6506496 | tf_op jit(solution)/shard_map/while/body/eval_jaxpr/whqk,wqhd->wkhd/dot_general | solution.py:22
  477.0 9.1 %fusion.139 = bf16[4,144,8,64]{1,3,2,0:T(8,128)(2,1)} fusion(bf16[4,144,8,64]{1,3,2,0:T(8,128)(2,1)S(1)} %copy-done.5, f32[4,8,144,144]{2,3,1,0:T(8,128)} %fusion.137, f32[4,8,144,144]{2,3,1,0:T(8,128)} %get-tuple-element.216, f32[4,8,144]{2,1,0:T(8,128)S(1)} %get-tuple-element.217), kind=kOutput, calls=%fused_computation.24.clone.1 | convolution fusion | flops 89879184 | bytes 6506496 | tf_op jit(solution)/shard_map/while/body/eval_jaxpr/whqk,wkhd->wqhd/dot_general | solution.py:22
  497.9 5.3 convolution_add_fusion.5
  515.9 2.5 convolution_convert_fusion.6
  528.6 5.7 fusion.138
  534.2 2.8 fusion.142
  543.6 2.8 convolution_add_fusion.6
  546.4 3.3 fusion.141
  551.1 4.6 fusion.137
  555.7 9.5 %fusion.140 = bf16[4,144,8,64]{1,3,2,0:T(8,128)(2,1)} fusion(bf16[4,144,8,64]{1,3,2,0:T(8,128)(2,1)} %copy.267, f32[4,8,144,144]{2,3,1,0:T(8,128)} %fusion.137, f32[4,8,144,144]{2,3,1,0:T(8,128)} %get-tuple-element.216, f32[4,8,144]{2,1,0:T(8,128)S(1)} %get-tuple-element.217), kind=kOutput, calls=%fused_computation.23.clone.1 | convolution fusion | flops 89879184 | bytes 6506496 | tf_op jit(solution)/shard_map/while/body/eval_jaxpr/whqk,wqhd->wkhd/dot_general | solution.py:22
  565.2 9.1 %fusion.139 = bf16[4,144,8,64]{1,3,2,0:T(8,128)(2,1)} fusion(bf16[4,144,8,64]{1,3,2,0:T(8,128)(2,1)S(1)} %copy-done.5, f32[4,8,144,144]{2,3,1,0:T(8,128)} %fusion.137, f32[4,8,144,144]{2,3,1,0:T(8,128)} %get-tuple-element.216, f32[4,8,144]{2,1,0:T(8,128)S(1)} %get-tuple-element.217), kind=kOutput, calls=%fused_computation.24.clone.1 | convolution fusion | flops 89879184 | bytes 6506496 | tf_op jit(solution)/shard_map/while/body/eval_jaxpr/whqk,wkhd->wqhd/dot_general | solution.py:22
  586.2 5.3 convolution_add_fusion.5
  596.6 7.8 %collective-permute-done.2 = bf16[2,2,24,6,512]{4,2,3,1,0:T(8,128)(2,1)S(1)} collective-permute-done((bf16[2,2,24,6,512]{4,2,3,1,0:T(8,128)(2,1)S(1)}, bf16[2,2,24,6,512]{4,2,3,1,0:T(8,128)(2,1)S(1)}, u32[]{:S(2)}, u32[]{:S(2)}) %collective-permute-start.2) | collective-permute-done | bytes 589856 | tf_op jit(solution)/shard_map/ppermute | solution.py:18
  607.1 18.3 %collective-permute-done.3 = bf16[2,2,3,48,512]{4,3,2,1,0:T(8,128)(2,1)} collective-permute-done((bf16[2,2,3,48,512]{4,3,2,1,0:T(8,128)(2,1)}, bf16[2,2,3,48,512]{4,3,2,1,0:T(8,128)(2,1)}, u32[]{:S(2)}, u32[]{:S(2)}) %collective-permute-start.3) | collective-permute-done | bytes 589856 | tf_op jit(solution)/shard_map/ppermute | solution.py:18
  626.5 4.2 fusion.47
  630.7 2.5 fusion.46
  633.2 118.3 %all-reduce.5.cloned.1.call-done = (f32[512,1536]{1,0:T(8,128)}, f32[512,512]{1,0:T(8,128)}) async-done(((f32[512,1536]{1,0:T(8,128)}, f32[512,512]{1,0:T(8,128)}), (f32[512,1536]{1,0:T(8,128)}, f32[512,512]{1,0:T(8,128)})) %all-reduce.5.cloned.1.call-update) | async-done | bytes 4194320
  (318 shorter events, 194.9 us)
Async XLA Ops:
  7.2 8.1 %copy-start.11 = (bf16[2,24,48,512]{3,2,1,0:T(8,128)(2,1)S(1)}, bf16[2,24,48,512]{3,2,1,0:T(8,128)(2,1)}, u32[]{:S(2)}) copy-start(bf16[2,24,48,512]{3,2,1,0:T(8,128)(2,1)} %param.6) | copy-start | bytes 7077892
  7.2 221.0 %all-gather.4.cloned.1.call-start = ((), (), s32[]{:S(2)}) async-start(), calls=%async_computation | async-start | bytes 1585152 | tf_op jit(solution)/shard_map/all_gather | solution.py:139
  7.9 743.5 %all-reduce.5.cloned.1.call-start = ((), (), s32[]{:S(2)}) async-start(), calls=%async_computation.1 | async-start | bytes 8388608
  9.1 18.4 %collective-permute-start = (bf16[2,2,3,48,512]{4,3,2,1,0:T(8,128)(2,1)S(1)}, bf16[2,2,3,48,512]{4,3,2,1,0:T(8,128)(2,1)S(1)}, u32[]{:S(2)}, u32[]{:S(2)}) collective-permute-start(bf16[2,2,3,48,512]{4,3,2,1,0:T(8,128)(2,1)S(1)} %pad_maximum_fusion.4), channel_id=1, source_target_pairs={{16,0},{32,16},{48,32},{64,48},{80,64},{96,80},{112,96},{0,112},{1... | collective-permute-start | bytes 1769480 | tf_op jit(solution)/shard_map/ppermute | solution.py:18
  16.7 2.9 slice-start
  19.6 8.5 %copy-start.8 = (bf16[2,21,48,512]{3,1,2,0:T(8,128)(2,1)}, bf16[2,21,48,512]{3,1,2,0:T(8,128)(2,1)S(1)}, u32[]{:S(2)}) copy-start(bf16[2,21,48,512]{3,1,2,0:T(8,128)(2,1)S(1)} %copy.230) | copy-start | bytes 6193156
  20.8 7.4 copy-start.6
  28.1 1.8 copy-start.13
  28.3 189.9 %collective-permute-start.1 = (bf16[2,2,24,6,512]{4,2,3,1,0:T(8,128)(2,1)S(1)}, bf16[2,2,24,6,512]{4,2,3,1,0:T(8,128)(2,1)S(1)}, u32[]{:S(2)}, u32[]{:S(2)}) collective-permute-start(bf16[2,2,24,6,512]{4,2,3,1,0:T(8,128)(2,1)S(1)} %pad_maximum_fusion.5), channel_id=1, source_target_pairs={{1,0},{2,1},{3,2},{4,3},{5,4},{6,5},{7,6},{8,7},{9,8},{10,9},{11,1... | collective-permute-start | bytes 1769480 | tf_op jit(solution)/shard_map/ppermute | solution.py:18
  213.4 2.1 copy-start.7
  243.9 2.7 copy-start.2
  267.0 5.6 copy-start.1
  280.6 3.0 copy-start
  292.9 9.5 %copy-start.5 = (bf16[4,144,8,64]{1,3,2,0:T(8,128)(2,1)S(1)}, bf16[4,144,8,64]{1,3,2,0:T(8,128)(2,1)}, u32[]{:S(2)}) copy-start(bf16[4,144,8,64]{1,3,2,0:T(8,128)(2,1)} %copy.263) | copy-start | bytes 1769476 | tf_op jit(solution)/shard_map/while
  318.7 2.6 copy-start.12
  326.7 1.1 copy-start.4
  326.7 2.3 copy-start.3
  329.0 2.7 copy-start.2
  352.1 5.7 copy-start.1
  365.7 4.2 copy-start
  379.2 9.5 %copy-start.5 = (bf16[4,144,8,64]{1,3,2,0:T(8,128)(2,1)S(1)}, bf16[4,144,8,64]{1,3,2,0:T(8,128)(2,1)}, u32[]{:S(2)}) copy-start(bf16[4,144,8,64]{1,3,2,0:T(8,128)(2,1)} %copy.263) | copy-start | bytes 1769476 | tf_op jit(solution)/shard_map/while
  405.0 2.6 copy-start.12
  415.0 1.1 copy-start.4
  415.0 2.3 copy-start.3
  417.3 2.7 copy-start.2
  440.3 5.7 copy-start.1
  453.9 4.2 copy-start
  467.5 9.5 %copy-start.5 = (bf16[4,144,8,64]{1,3,2,0:T(8,128)(2,1)S(1)}, bf16[4,144,8,64]{1,3,2,0:T(8,128)(2,1)}, u32[]{:S(2)}) copy-start(bf16[4,144,8,64]{1,3,2,0:T(8,128)(2,1)} %copy.263) | copy-start | bytes 1769476 | tf_op jit(solution)/shard_map/while
  493.3 2.6 copy-start.12
  503.2 1.1 copy-start.4
  503.2 2.3 copy-start.3
  505.5 2.7 copy-start.2
  528.6 5.7 copy-start.1
  542.2 4.2 copy-start
  555.7 9.5 %copy-start.5 = (bf16[4,144,8,64]{1,3,2,0:T(8,128)(2,1)S(1)}, bf16[4,144,8,64]{1,3,2,0:T(8,128)(2,1)}, u32[]{:S(2)}) copy-start(bf16[4,144,8,64]{1,3,2,0:T(8,128)(2,1)} %copy.263) | copy-start | bytes 1769476 | tf_op jit(solution)/shard_map/while
  581.5 2.6 copy-start.12
  591.4 1.1 copy-start.4
  591.4 2.3 copy-start.3
  596.5 7.9 %collective-permute-start.2 = (bf16[2,2,24,6,512]{4,2,3,1,0:T(8,128)(2,1)S(1)}, bf16[2,2,24,6,512]{4,2,3,1,0:T(8,128)(2,1)S(1)}, u32[]{:S(2)}, u32[]{:S(2)}) collective-permute-start(bf16[2,2,24,6,512]{4,2,3,1,0:T(8,128)(2,1)S(1)} %copy.211), channel_id=1, source_target_pairs={{15,0},{0,1},{1,2},{2,3},{3,4},{4,5},{5,6},{6,7},{7,8},{8,9},{9,10... | collective-permute-start | bytes 1769480 | tf_op jit(solution)/shard_map/ppermute | solution.py:18
  596.6 8.1 %copy-start.9 = (bf16[4,2,6,48,512]{4,3,2,0,1:T(8,128)(2,1)S(1)}, bf16[4,2,6,48,512]{4,3,2,0,1:T(8,128)(2,1)}, u32[]{:S(2)}) copy-start(bf16[4,2,6,48,512]{4,3,2,0,1:T(8,128)(2,1)} %get-tuple-element.60) | copy-start | bytes 7077892
  604.4 1.7 copy-start.10
  607.1 18.3 %collective-permute-start.3 = (bf16[2,2,3,48,512]{4,3,2,1,0:T(8,128)(2,1)}, bf16[2,2,3,48,512]{4,3,2,1,0:T(8,128)(2,1)}, u32[]{:S(2)}, u32[]{:S(2)}) collective-permute-start(bf16[2,2,3,48,512]{4,3,2,1,0:T(8,128)(2,1)} %pad_maximum_fusion.6), channel_id=1, source_target_pairs={{112,0},{0,16},{16,32},{32,48},{48,64},{64,80},{80,96},{96,112},{1... | collective-permute-start | bytes 1769480 | tf_op jit(solution)/shard_map/ppermute | solution.py:18
Sparse Core Ops, SparseCore 0:
  9.7 199.8 all-gather.3
  596.8 154.6 all-reduce.4
where the time goes:
time: 768 us; the launch traced here: 761 us
  matrix products  197 us (26%)
  blocking collectives  181 us (24%)
  local copies, waits for them, and re-layouts  159 us (21%)
  waiting for transfers between devices  152 us (20%)
  other arithmetic  36.5 us (5%)
  between operations  14.7 us (2%)
  loops' own time  13.4 us (2%)
  starting transfers between devices  7.91 us (1%)
    all_gather x1, blocking collectives, body(): lax.all_gather(out_weight, ('lat', 'lon'), axis=0, tiled=True)  181 us
    unnamed x3, waiting for transfers between devices  119 us
    dot_general x20, matrix products, product(): return jnp.einsum(pattern, left, right, preferred_element_type=jnp.float32)  117 us
    ppermute x4, waiting for transfers between devices, passed_along(): return lax.ppermute(block, axis, route)  32.8 us
    dot_general x8, matrix products, transposed_times(): lax.dot_general(left, right, (((0,), (0,)), ((), ())), preferred_element_...  29.1 us
    sub x4, matrix products, slab_step(): shifted_exp = jnp.exp(scores - maximum)  22.6 us
    dot_general x8, matrix products, matmul(): return jnp.dot(left, right, preferred_element_type=jnp.float32)  19.6 us
  transfers between devices with their start and end apart: 6, of which 4 were waited for; matrix products, arithmetic and copies ran while one was open for 4% of the time, Pallas kernels for 0%

commit v1 on v0

v1 whole, which is shorter than its diff:
```python
import functools
import math

import jax
import jax.numpy as jnp
from jax import lax
from jax.experimental import pallas as pl
from jax.experimental.pallas import tpu as pltpu
from jax.sharding import PartitionSpec as P

C = 512
HD = 64
WIN_LAT = 6
WIN_LON = 12
LEVELS = 2
PIECES = LEVELS * WIN_LAT
TOK = PIECES * WIN_LON
SLABS = 4
ACROSS = 4
WINDOWS = SLABS * ACROSS
TOKENS = WINDOWS * TOK
SLAB = ACROSS * TOK
HALF_ROWS = 3
HALF_COLS = 6
ROWS = 24
COLS = 48
TILES = ROWS // 2
HALF = 2 * C
BF = jnp.bfloat16
F32 = jnp.float32


def nn(a, b):
    return lax.dot_general(a, b, (((1,), (0,)), ((), ())), preferred_element_type=F32)


def nt(a, b):
    return lax.dot_general(a, b, (((1,), (1,)), ((), ())), preferred_element_type=F32)


def tn(a, b):
    return lax.dot_general(a, b, (((0,), (0,)), ((), ())), preferred_element_type=F32)


MESH = pl.DeviceIdType.MESH
GROUP = [(a, b, c) for a in range(2) for b in range(2) for c in range(2)][1:]


class Place:
    def __init__(self):
        self.lat, self.lon = lax.axis_index("lat"), lax.axis_index("lon")
        self.x_hi, self.y = self.lat // 4, self.lat % 4
        self.z, self.x_lo, self.core = self.lon // 4, (self.lon // 2) % 2, self.lon % 2

    def mate(self, flips):
        a, b, c = (v + f - 2 * v * f for v, f in zip((self.x_hi, self.x_lo, self.core), flips))
        return (a * 4 + self.y, self.z * 4 + b * 2 + c)

    def along(self, axis, step):
        if axis == "y":
            return (self.x_hi * 4 + (self.y + step) % 4, self.lon)
        return (self.lat, (self.z + step) % 4 * 4 + self.lon % 4)

    def shifted(self, rows, cols):
        return ((self.lat + rows + 8) % 8, (self.lon + cols + 16) % 16)


def greet(senders):
    barrier = pltpu.get_barrier_semaphore()
    for device in senders:
        pl.semaphore_signal(barrier, inc=1, device_id=device, device_id_type=MESH)
    pl.semaphore_wait(barrier, len(senders))


def remote(src, dst, sems, slot, device):
    return pltpu.make_async_remote_copy(
        src_ref=src, dst_ref=dst, send_sem=sems.at[0, slot], recv_sem=sems.at[1, slot],
        device_id=device, device_id_type=MESH)


def partners(place):
    return ([place.mate(f) for f in GROUP]
            + [place.along("y", s) for s in (1, 2, 3)] + [place.along("z", s) for s in (1, 2, 3)])


def fused_kernel(
    factor,
    lat_ref, cot_ref, shard_ref,
    out_ref, grad_ref, back_rows, back_cols, back_corner, sum_qkv, sum_out,
    grid, cols_in, corner_in, strip, corner_strip,
    shard_in, loose, weights,
    rows, window, wide, x_w, inv_w, normed, ctx, gctx, qkv,
    lhs, lhs_t, gp, bias, bias_tail,
    outgoing, rows_out, cols_out, corner_out,
    terms, from_mate, total, sent, from_near, from_far, relay, total2, sent2, from_second, sent3, from_group,
    grid_sems, halo_sems, group_sems, axis_sems, mate_sems, out_sems, back_sems, sum_sems, final_sems,
):
    place = Place()
    loads = [pltpu.make_async_copy(ref, grid.at[i, :, :ROWS], grid_sems.at[i]) for i, ref in enumerate((lat_ref, cot_ref))]
    for load in loads:
        load.start()
    near = [place.shifted(1, 0), place.shifted(0, 1), place.shifted(1, 1),
            place.shifted(-1, 0), place.shifted(0, -1), place.shifted(-1, -1)]
    barrier = pltpu.get_barrier_semaphore()
    for device in partners(place) + near:
        pl.semaphore_signal(barrier, inc=1, device_id=device, device_id_type=MESH)
    down, right, across_down, up, left, across_up = near

    last = lax.axis_index("lat") == lax.axis_size("lat") - 1
    key = lax.broadcasted_iota(jnp.int32, (TOK, 128), 0)
    query = lax.broadcasted_iota(jnp.int32, (TOK, 128), 1)

    def flag(token):
        row = token // WIN_LON
        return jnp.where(row >= WIN_LAT, row - WIN_LAT, row) >= HALF_ROWS

    seam = jnp.where(last, -1e30, 0.0).astype(F32)
    bias[0] = jnp.zeros((TOK, 128), F32)
    bias_tail[0] = jnp.zeros((TOK, 128), F32)
    bias[1] = jnp.where(flag(key) != flag(query), seam, 0.0)
    bias_tail[1] = jnp.where(flag(key), 0.0, seam)

    for which in range(2):
        loads[which].wait()
        for level in range(LEVELS):
            def columns(row):
                return grid[which, level, row, :16].astype(F32)[:8]
            for tile in range(TILES - 1):
                first = HALF_ROWS + 2 * tile
                strip[which, level, tile] = jnp.concatenate(
                    [columns(first), columns(min(first + 1, ROWS - 1))], 0).astype(BF)
            corner_strip[which, level, 0] = jnp.concatenate([columns(0), columns(0)], 0).astype(BF)
            corner_strip[which, level, 1] = jnp.concatenate([columns(1), columns(2)], 0).astype(BF)
    pl.semaphore_wait(barrier, len(partners(place)) + len(near))

    here = (place.x_hi, place.x_lo, place.core)
    group = []
    for slot, flips in enumerate(GROUP):
        copy = remote(shard_ref.at[place.core if flips[2] == 0 else 1 - place.core],
                      shard_in.at[here], group_sems, slot, place.mate(flips))
        copy.start()
        group.append(copy)
    shard_in[here] = shard_ref[place.core]
    halo_cols, halo_rows = [], []
    for which in range(2):
        halo_cols.append(remote(strip.at[which], cols_in.at[which, :, : TILES - 1], halo_sems, which, left))
        halo_rows.append(remote(corner_strip.at[which], corner_in.at[which], halo_sems, 2 + which, across_up))
        for level in range(LEVELS):
            halo_rows.append(remote(grid.at[which, level, :HALF_ROWS], grid.at[which, level, ROWS:], halo_sems,
                                    4 + 2 * which + level, up))
    for copy in halo_cols:
        copy.start()

    for copy in group:
        copy.wait()
    for x_hi in range(2):
        for b in range(2):
            for c in range(2):
                for lane_tile in range(2):
                    line = 16 * (2 * b + c)
                    loose[x_hi, lane_tile, line : line + 16] = (
                        shard_in[x_hi, b, c][:, 128 * lane_tile : 128 * lane_tile + 128].astype(F32))
    for core in range(2):
        half = slice(HALF * core, HALF * (core + 1))

        @pl.when(place.core == core)
        def _():
            for x_hi in range(2):
                for block in range(4):
                    for lane_tile in range(2):
                        start = HALF * core + 256 * block + 128 * lane_tile
                        weights[x_hi, place.y, place.z, :, start : start + 128] = (
                            loose[x_hi, lane_tile, pl.ds(block, 16, stride=4)].astype(BF))
            first, second = ("z", "y") if core == 0 else ("y", "z")
            small = weights.at[:, place.y, place.z, :, half]
            copies = [remote(small, small, axis_sems, step - 1, place.along(first, step)) for step in (1, 2, 3)]
            for copy in copies:
                copy.start()
            for copy in copies:
                copy.wait()
            mine = place.y if core == 0 else place.z

            def block(step, x_hi=slice(None)):
                index = (mine + step) % 4
                return weights.at[x_hi, index, :, :, half] if core == 0 else weights.at[x_hi, :, index, :, half]

            other = place.mate((0, 0, 1))
            ahead = remote(block(0), block(0), axis_sems, 3, place.along(second, 1))
            behind = remote(block(0), block(0), axis_sems, 4, place.along(second, 3))
            ahead.start()
            behind.start()
            mates = [remote(block(0), block(0), mate_sems, 0, other)]
            mates[0].start()
            ahead.wait()
            relays = [remote(block(3, 0), block(3, 0), axis_sems, 5, place.along(second, 1))]
            relays[0].start()
            behind.wait()
            relays.append(remote(block(1, 1), block(1, 1), axis_sems, 6, place.along(second, 3)))
            relays[1].start()
            mates.append(remote(block(3), block(3), mate_sems, 1, other))
            mates.append(remote(block(1), block(1), mate_sems, 2, other))
            mates[1].start()
            mates[2].start()
            for copy in relays:
                copy.wait()
            mates.append(remote(block(2), block(2), mate_sems, 3, other))
            mates[3].start()
            for copy in mates:
                copy.wait()
    for copy in halo_rows:
        copy.start()
    for copy in halo_cols:
        copy.wait()
    w_ref = weights.reshape(C, 4 * C)

    lane = lax.broadcasted_iota(jnp.int32, (1, 128), 1)
    low = (lane < HD).astype(F32).astype(BF)
    high = (lane >= HD).astype(F32).astype(BF)
    low_lanes = lax.broadcasted_iota(jnp.int32, (128, 128), 1) < HD
    low_lanes16 = lax.broadcasted_iota(jnp.int32, (16, 128), 1) < HD

    def spread(tail):
        zero = jnp.zeros((16, 128), BF)
        lines = []
        for head in range(8):
            pair = head // 2
            mine = tail[:, 128 * pair : 128 * (pair + 1)] * (low if head % 2 == 0 else high)
            lines.append(jnp.concatenate([mine if p == pair else zero for p in range(4)], 1))
        return jnp.concatenate(lines, 0)

    def gather(full, pair):
        cols = slice(128 * pair, 128 * (pair + 1))
        return jnp.where(low_lanes16, full[32 * pair : 32 * pair + 16, cols], full[32 * pair + 16 : 32 * pair + 32, cols])

    def softmax_both(scores, grad_att):
        top = jnp.max(scores, 0, keepdims=True)
        raised = jnp.exp(scores - top)
        att = raised * (1.0 / jnp.sum(raised, 0, keepdims=True))
        weighed = grad_att * att
        inner = jnp.sum(weighed, 0, keepdims=True)
        return att.astype(BF), (weighed - att * inner).astype(BF)

    def load_slab(slab, base):
        for which in range(2):
            for level in range(LEVELS):
                for row in range(WIN_LAT):
                    piece = level * WIN_LAT + row
                    rows[which, piece, :COLS] = grid[which, level, slab * WIN_LAT + row + HALF_ROWS].astype(F32)
                    half = row % 2
                    rows[which, piece, COLS:] = (
                        cols_in[which, level, 3 * slab + row // 2].astype(F32)[8 * half : 8 * half + 8])
        for across in range(ACROSS):
            start = HALF_COLS + WIN_LON * across
            part = slice(across * TOK, (across + 1) * TOK)
            for which in range(2):
                for piece in range(PIECES):
                    window[which, WIN_LON * piece : WIN_LON * (piece + 1)] = rows[which, piece, start : start + WIN_LON]
            widened = window[0]
            centred = widened - jnp.mean(widened, -1, keepdims=True)
            inv = lax.rsqrt(jnp.mean(centred * centred, -1, keepdims=True) + 1e-05)
            x_w[part] = widened.astype(BF)
            inv_w[part] = inv
            normed[part] = (centred * inv).astype(BF)
            gp[pl.ds(pl.multiple_of(base + across * TOK, 16), TOK), 3 * C :] = window[1].astype(BF)

    def attend(base, seam_slab):
        offset = bias[seam_slab]
        offset = jnp.concatenate([offset, offset], 1)
        units = []
        for across in range(ACROSS):
            token = across * TOK
            main, tail, whole = slice(token, token + 128), slice(token + 128, token + TOK), slice(token, token + TOK)
            keys = qkv[whole, C : 2 * C]
            values = qkv[whole, 2 * C :]
            units.append((across, None, spread(qkv[tail, :C]), spread(gctx[tail]), keys, values))
            for pair in range(4):
                cols = slice(128 * pair, 128 * (pair + 1))
                q = qkv[main, cols]
                g = gctx[main, cols]
                q_both = jnp.concatenate([q * low, q * high], 0)
                g_both = jnp.concatenate([g * low, g * high], 0)
                units.append((across, pair, q_both, g_both, keys[:, cols], values[:, cols]))
        products = [(nt(k, q), nt(v, g)) for _, _, q, g, k, v in units]
        softened = []
        for unit, (scores, grad_att) in zip(units, products):
            softened.append(softmax_both(scores + (bias_tail[seam_slab] if unit[1] is None else offset), grad_att))
        made = [(tn(a, v), tn(s, k)) for (a, s), (_, _, q, g, k, v) in zip(softened, units)]
        made2 = [(nn(s, q), nn(a, g)) for (a, s), (_, _, q, g, k, v) in zip(softened, units)]
        for unit, (context, grad_q), (grad_k, grad_v) in zip(units, made, made2):
            across, pair = unit[:2]
            if pair is None:
                ctx_tail, gq_tail, gk_tail, gv_tail = context, grad_q, grad_k, grad_v
                continue
            token = across * TOK
            cols = slice(128 * pair, 128 * (pair + 1))
            g_main = pl.ds(pl.multiple_of(base + token, 16), 128)
            g_tail = pl.ds(pl.multiple_of(base + token + 128, 16), 16)
            g_whole = pl.ds(pl.multiple_of(base + token, 16), TOK)
            ctx[token : token + 128, cols] = jnp.where(low_lanes, context[:128], context[128:]).astype(BF)
            ctx[token + 128 : token + TOK, cols] = gather(ctx_tail, pair).astype(BF)
            gp[g_main, cols] = (jnp.where(low_lanes, grad_q[:128], grad_q[128:]) * HD ** -0.5).astype(BF)
            gp[g_tail, cols] = (gather(gq_tail, pair) * HD ** -0.5).astype(BF)
            gp[g_whole, C + 128 * pair : C + 128 * (pair + 1)] = (grad_k + gk_tail[:, cols]).astype(BF)
            gp[g_whole, 2 * C + 128 * pair : 2 * C + 128 * (pair + 1)] = (grad_v + gv_tail[:, cols]).astype(BF)

    def store_slab(slab):
        for which in range(2):
            for level in range(LEVELS):
                for row in range(WIN_LAT):
                    piece = level * WIN_LAT + row
                    for across in range(ACROSS):
                        start = HALF_COLS + WIN_LON * across
                        token = across * TOK + piece * WIN_LON
                        rows[which, piece, start : start + WIN_LON] = wide[which, token : token + WIN_LON]
                    outgoing[slab, which, level, row] = rows[which, piece, :COLS].astype(BF)
                for tile in range(3):
                    piece = level * WIN_LAT + 2 * tile
                    cols_out[which, level, 3 * slab + tile] = jnp.concatenate(
                        [rows[which, piece, COLS:], rows[which, piece + 1, COLS:]], 0).astype(BF)

    def out_copies(slab):
        first = slab * WIN_LAT + HALF_ROWS
        return [pltpu.make_async_copy(outgoing.at[slab, which], target.at[:, pl.ds(first, WIN_LAT)], out_sems.at[slab, which])
                for which, target in enumerate((out_ref, grad_ref))]

    def out_copies_last():
        return [pltpu.make_async_copy(outgoing.at[SLABS - 1, which, :, :HALF_ROWS], target.at[:, ROWS - HALF_ROWS :],
                                      out_sems.at[SLABS - 1, which])
                for which, target in enumerate((out_ref, grad_ref))]

    def back_copies(slab):
        return [remote(cols_out.at[which, :, pl.ds(3 * slab, 3)], back_cols.at[which, :, pl.ds(3 * slab, 3)], back_sems,
                       2 * slab + which, right) for which in range(2)]

    def back_copies_last():
        copies = []
        for which in range(2):
            copies.append(remote(outgoing.at[SLABS - 1, which, :, HALF_ROWS:], back_rows.at[which], back_sems, 8 + which, down))
            copies.append(remote(cols_out.at[which, :, TILES - 2 :], back_corner.at[which], back_sems, 10 + which, across_down))
        return copies

    @pl.loop(0, SLABS)
    def _(step):
        slab = step + (step // 2) * (1 - 2 * (step % 2))
        base = pl.multiple_of(step * SLAB, 64)

        @pl.when(step == 2)
        def _():
            for copy in halo_rows:
                copy.wait()
            for which in range(2):
                for level in range(LEVELS):
                    cols_in[which, level, TILES - 2] = jnp.concatenate(
                        [cols_in[which, level, TILES - 2].astype(F32)[:8], corner_in[which, level, 0].astype(F32)[8:]], 0).astype(BF)
                    cols_in[which, level, TILES - 1] = corner_in[which, level, 1]

        load_slab(slab, base)
        block = normed[...]
        lhs[0, pl.ds(pl.multiple_of((step % 2) * SLAB, 64), SLAB)] = block
        for third in range(3):
            cols = slice(C * third, C * (third + 1))
            projected = nn(block, w_ref[:, cols]).astype(BF)
            qkv[:, cols] = projected * BF(HD ** -0.5) if third == 0 else projected
        gctx[...] = nt(gp[pl.ds(base, SLAB), 3 * C :], w_ref[:, 3 * C :]).astype(BF)
        attend(base, step // 2 * (1 - step % 2))
        context = ctx[...]
        lhs[1, pl.ds(pl.multiple_of((step % 2) * SLAB, 64), SLAB)] = context
        wide[0] = x_w[...].astype(F32) + nn(context, w_ref[:, 3 * C :])
        grad_normed = nt(gp[pl.ds(base, SLAB), : 3 * C], w_ref[:, : 3 * C])
        standard = normed[...].astype(F32)
        first_mean = jnp.mean(grad_normed, -1, keepdims=True)
        second_mean = jnp.mean(grad_normed * standard, -1, keepdims=True)
        wide[1] = inv_w[...] * (grad_normed - first_mean - standard * second_mean) + gp[pl.ds(base, SLAB), 3 * C :].astype(F32)
        store_slab(slab)
        for copy in back_copies(slab):
            copy.start()

        @pl.when(step == 2)
        def _():
            for copy in out_copies_last() + back_copies_last():
                copy.start()

        @pl.when(step != 2)
        def _():
            for copy in out_copies(slab):
                copy.start()

        @pl.when(step % 2 == 1)
        def _():
            for which in range(2):
                lhs_t[which, :, pl.ds(pl.multiple_of(step // 2 * (2 * SLAB), 128), 2 * SLAB)] = lhs[which].T

    other = place.mate((0, 0, 1))

    def columns_of(half, part):
        return (half * 2 + part) % 4

    def product(block):
        return nn(lhs_t[block // 3], gp[:, pl.ds(pl.multiple_of(block * C, 128), C)])

    def mate_copy(part):
        return remote(terms.at[part], from_mate.at[part], sum_sems, part, other)

    @pl.loop(0, 2)
    def _(part):
        terms[part] = product(columns_of(1 - place.core, part)).astype(BF).reshape(2, 4, 4, 16, C)
        mate_copy(part).start()

    @pl.loop(0, 2)
    def _(part):
        mate_copy(part).wait()
        added = product(columns_of(place.core, part)) + from_mate[part].reshape(C, C).astype(F32)
        total[part] = added.reshape(2, 4, 4, 16, C)
        sent[part] = added.astype(BF).reshape(2, 4, 4, 16, C)

    for core in range(2):
        @pl.when(place.core == core)
        def _():
            first, second = ("y", "z") if core == 0 else ("z", "y")
            mine = place.y if core == 0 else place.z

            def block(ref, step, x_hi):
                index = (mine + step) % 4
                return ref.at[:, x_hi, index] if core == 0 else ref.at[:, x_hi, :, index]

            ahead, behind = place.along(first, 1), place.along(first, 3)
            far = [remote(block(sent, 2, 0), from_far.at[0], sum_sems, 2, ahead),
                   remote(block(sent, 2, 1), from_far.at[1], sum_sems, 3, behind)]
            plain = [remote(block(sent, 1, 1), from_near.at[0, 1], sum_sems, 4, ahead),
                     remote(block(sent, 3, 0), from_near.at[1, 0], sum_sems, 5, behind)]
            for copy in far + plain:
                copy.start()
            summed = []
            for way, (step, x_hi, device) in enumerate(((1, 0, ahead), (3, 1, behind))):
                far[way].wait()
                relay[way] = (block(total, step, x_hi)[...] + from_far[way].astype(F32)).astype(BF)
                summed.append(remote(relay.at[way], from_near.at[way, x_hi], sum_sems, 6 + way, device))
                summed[way].start()
            for copy in plain + summed:
                copy.wait()
            for x_hi in range(2):
                added = block(total, 0, x_hi)[...] + from_near[0, x_hi].astype(F32) + from_near[1, x_hi].astype(F32)
                total2[x_hi] = added
                sent2[x_hi] = added.astype(BF)
            mine2 = place.z if core == 0 else place.y
            copies = [remote(sent2.at[:, :, (mine2 + step) % 4], from_second.at[step - 1], sum_sems, 8 + step - 1,
                             place.along(second, step)) for step in (1, 2, 3)]
            for copy in copies:
                copy.start()
            for copy in copies:
                copy.wait()
            added = total2[:, :, mine2]
            for step in range(3):
                added = added + from_second[step].astype(F32)
            sent3[...] = added.astype(BF)

    copies = []
    for slot, flips in enumerate(GROUP):
        target = place.x_hi if flips[0] == 0 else 1 - place.x_hi
        copies.append(remote(sent3.at[target], from_group.at[here], final_sems, slot, place.mate(flips)))
    for copy in copies:
        copy.start()
    from_group[here] = sent3[place.x_hi]
    for copy in copies:
        copy.wait()
    position = place.x_lo * 2 + place.core
    for block in range(4):
        added = from_group[0, 0, block // 2, block % 2].astype(F32)
        for a, b in ((0, 1), (1, 0), (1, 1)):
            added = added + from_group[a, b, block // 2, block % 2].astype(F32)
        picked = added[:4]
        for i in range(1, 4):
            picked = jnp.where(position == i, added[4 * i : 4 * i + 4], picked)
        if block < 3:
            sum_qkv[:, C * block : C * (block + 1)] = picked * factor
        else:
            sum_out[...] = picked * factor
    for slab in range(SLABS):
        for copy in back_copies(slab):
            copy.wait()
    for slab in range(SLABS - 1):
        for copy in out_copies(slab):
            copy.wait()
    for copy in out_copies_last() + back_copies_last():
        copy.wait()


def fused(latent, cotangent, shard, factor):
    anywhere = pl.BlockSpec(memory_space=pl.ANY)
    whole = pl.BlockSpec(memory_space=pltpu.VMEM)
    grid_shape = jax.ShapeDtypeStruct((LEVELS, ROWS, COLS, C), BF)
    dma = pltpu.SemaphoreType.DMA
    return pl.pallas_call(
        functools.partial(fused_kernel, factor),
        out_shape=(
            grid_shape,
            grid_shape,
            jax.ShapeDtypeStruct((2, LEVELS, HALF_ROWS, COLS, C), BF),
            jax.ShapeDtypeStruct((2, LEVELS, TILES, 16, C), BF),
            jax.ShapeDtypeStruct((2, LEVELS, 2, 16, C), BF),
            jax.ShapeDtypeStruct((4, 3 * C), F32),
            jax.ShapeDtypeStruct((4, C), F32),
        ),
        in_specs=[anywhere, anywhere, whole],
        out_specs=(anywhere,) * 5 + (whole,) * 2,
        scratch_shapes=[
            pltpu.VMEM((2, LEVELS, ROWS + HALF_ROWS, COLS, C), BF),
            pltpu.VMEM((2, LEVELS, TILES, 16, C), BF),
            pltpu.VMEM((2, LEVELS, 2, 16, C), BF),
            pltpu.VMEM((2, LEVELS, TILES - 1, 16, C), BF),
            pltpu.VMEM((2, LEVELS, 2, 16, C), BF),
            pltpu.VMEM((2, 2, 2, 16, 256), BF),
            pltpu.VMEM((2, 2, 64, 128), F32),
            pltpu.VMEM((2, 4, 4, 16, 4 * C), BF),
            pltpu.VMEM((2, PIECES, COLS + 8, C), F32),
            pltpu.VMEM((2, TOK, C), F32),
            pltpu.VMEM((2, SLAB, C), F32),
            pltpu.VMEM((SLAB, C), BF),
            pltpu.VMEM((SLAB, 1), F32),
            pltpu.VMEM((SLAB, C), BF),
            pltpu.VMEM((SLAB, C), BF),
            pltpu.VMEM((SLAB, C), BF),
            pltpu.VMEM((SLAB, 3 * C), BF),
            pltpu.VMEM((2, 2 * SLAB, C), BF),
            pltpu.VMEM((2, C, TOKENS), BF),
            pltpu.VMEM((TOKENS, 4 * C), BF),
            pltpu.VMEM((2, TOK, 128), F32),
            pltpu.VMEM((2, TOK, 128), F32),
            pltpu.VMEM((SLABS, 2, LEVELS, WIN_LAT, COLS, C), BF),
            pltpu.VMEM((8, 128), F32),
            pltpu.VMEM((2, LEVELS, TILES, 16, C), BF),
            pltpu.VMEM((8, 128), F32),
            pltpu.VMEM((2, 2, 4, 4, 16, C), BF),
            pltpu.VMEM((2, 2, 4, 4, 16, C), BF),
            pltpu.VMEM((2, 2, 4, 4, 16, C), F32),
            pltpu.VMEM((2, 2, 4, 4, 16, C), BF),
            pltpu.VMEM((2, 2, 2, 4, 16, C), BF),
            pltpu.VMEM((2, 2, 4, 16, C), BF),
            pltpu.VMEM((2, 2, 4, 16, C), BF),
            pltpu.VMEM((2, 2, 4, 16, C), F32),
            pltpu.VMEM((2, 2, 4, 16, C), BF),
            pltpu.VMEM((3, 2, 2, 16, C), BF),
            pltpu.VMEM((2, 2, 16, C), BF),
            pltpu.VMEM((2, 2, 2, 2, 16, C), BF),
            dma((2,)),
            dma((2, 8)),
            dma((2, 7)),
            dma((2, 7)),
            dma((2, 4)),
            dma((SLABS, 2)),
            dma((2, 12)),
            dma((2, 11)),
            dma((2, 7)),
        ],
        compiler_params=pltpu.CompilerParams(
            collective_id=0, has_side_effects=True, vmem_limit_bytes=62 * 2**20),
        name="layer",
    )(latent, cotangent, shard)


def merge_kernel(out_in, grad_in, hr_ref, hc_ref, hd_ref, out_ref, grad_ref, edge, top, sems):
    del out_in, grad_in
    outs = (out_ref, grad_ref)
    loads = [pltpu.make_async_copy(ref.at[:, HALF_ROWS:, :16], edge.at[i], sems.at[i]) for i, ref in enumerate(outs)]
    for load in loads:
        load.start()
    column = lax.broadcasted_iota(jnp.int32, (16, C), 0)
    blank = jnp.zeros((8, C), F32)
    stores = []
    for which in range(2):
        loads[which].wait()
        for level in range(LEVELS):
            for row in range(ROWS):
                line = (row - HALF_ROWS) % ROWS
                ref = hc_ref if row >= HALF_ROWS else hd_ref
                tile = line // 2 if row >= HALF_ROWS else line // 2 - (TILES - 2)
                half = line % 2
                halo = jnp.concatenate([ref[which, level, tile].astype(F32)[8 * half : 8 * half + 8], blank], 0)
                if row >= HALF_ROWS:
                    own = edge[which, level, row - HALF_ROWS].astype(F32)
                    edge[which, level, row - HALF_ROWS] = jnp.where(column < HALF_COLS, halo, own).astype(BF)
                else:
                    own = hr_ref[which, level, row, :16].astype(F32)
                    top[which, level, row, :16] = jnp.where(column < HALF_COLS, halo, own).astype(BF)
                    top[which, level, row, 16:] = hr_ref[which, level, row, 16:]
        stores.append(pltpu.make_async_copy(edge.at[which], outs[which].at[:, HALF_ROWS:, :16], sems.at[which]))
        stores.append(pltpu.make_async_copy(top.at[which], outs[which].at[:, :HALF_ROWS], sems.at[2 + which]))
        for store in stores[-2:]:
            store.start()
    for store in stores:
        store.wait()


def merge(out, grad, row_strip, col_strip, corner):
    anywhere = pl.BlockSpec(memory_space=pl.ANY)
    whole = pl.BlockSpec(memory_space=pltpu.VMEM)
    grid_shape = jax.ShapeDtypeStruct((LEVELS, ROWS, COLS, C), BF)
    return pl.pallas_call(
        merge_kernel,
        out_shape=(grid_shape, grid_shape),
        in_specs=[anywhere, anywhere, whole, whole, whole],
        out_specs=(anywhere, anywhere),
        scratch_shapes=[
            pltpu.VMEM((2, LEVELS, ROWS - HALF_ROWS, 16, C), BF),
            pltpu.VMEM((2, LEVELS, HALF_ROWS, COLS, C), BF),
            pltpu.SemaphoreType.DMA((4,)),
        ],
        input_output_aliases={0: 0, 1: 1},
        compiler_params=pltpu.CompilerParams(vmem_limit_bytes=32 * 2**20),
        name="merge",
    )(out, grad, row_strip, col_strip, corner)


def body(latent, cotangent, qkv_weight, out_weight):
    pieces = jnp.concatenate([qkv_weight, out_weight], 1)
    shard = pieces.reshape(4, 2, 4, 256).transpose(1, 0, 2, 3).reshape(2, 16, 256)
    total_tokens = TOKENS * lax.axis_size("lat") * lax.axis_size("lon")
    out, grad, rows_in, cols_in, corner, sum_qkv, sum_out = fused(
        latent, cotangent, shard, 1.0 / math.sqrt(total_tokens))
    out, grad = merge(out, grad, rows_in, cols_in, corner)
    return out, grad, sum_qkv, sum_out


def solution(mesh):
    grid = P(None, "lat", "lon", None)
    rows = P(("lat", "lon"), None)
    specs = (grid, grid, rows, rows)
    return jax.shard_map(body, mesh=mesh, in_specs=specs, out_specs=specs, check_vma=False)
```

time: 768 us -> 110 us (0.14)
  matrix products: 197 us -> 0 us
  blocking collectives: 181 us -> 0 us
  waiting for transfers between devices: 152 us -> 0 us
  local copies, waits for them, and re-layouts: 159 us -> 11.1 us
  Pallas kernels: 0 us -> 97.3 us
  other arithmetic: 36.5 us -> 0.74 us
  between operations: 14.7 us -> 0.68 us
  loops' own time: 13.4 us -> 0 us
  starting transfers between devices: 7.91 us -> 0 us
    all_gather x1 -> x0, blocking collectives: 181 us -> none  [body(): lax.all_gather(out_weight, ('lat', 'lon'), axis=0, tiled=True)]
    dot_general x44 -> x0, matrix products: 174 us -> none  [the longest x20 117 us: product(): return jnp.einsum(pattern, left, right, preferred_element_type=jnp.float32)]
    unnamed x3 -> x0, waiting for transfers between devices: 119 us -> none
    pallas_call x0 -> x2, Pallas kernels: none -> 97.3 us  [the longest x1 96.8 us: fused(): pl.pallas_call(functools.partial(fused_kernel, factor), out_shape=(grid_s...]
    reshape x60 -> x3, local copies, waits for them, and re-layouts: 67.9 us -> 0.64 us  [body(): pieces.reshape(4, 2, 4, 256).transpose(1, 0, 2, 3).reshape(2, 16, 256)]
    ppermute x4 -> x0, waiting for transfers between devices: 32.8 us -> none  [passed_along(): return lax.ppermute(block, axis, route)]
    convert_element_type x24 -> x0, local copies, waits for them, and re-layouts: 24.4 us -> none  [the longest x4 8.16 us: slab_step(): product('whqk,wkhd->wqhd', grad_scores, key_heads).astype(jnp.bfloat16)]
    sub x4 -> x0, matrix products: 22.6 us -> none  [slab_step(): shifted_exp = jnp.exp(scores - maximum)]
  transfers between devices with their start and end apart: 6 -> 0, of which waited for: 4 -> 0; matrix products, arithmetic and copies ran while one was open for 4% -> 0% of each run, Pallas kernels for 0% -> 0%
where the time goes in v1:
time: 110 us
  Pallas kernels  97.3 us (88%)
  local copies, waits for them, and re-layouts  11.1 us (10%)
    pallas_call x1, Pallas kernels, fused(): pl.pallas_call(functools.partial(fused_kernel, factor), out_shape=(grid_s...  96.8 us
    unnamed x18, local copies, waits for them, and re-layouts  10.4 us

profile of v1, /device:TPU:1, one launch (start us, length us, event | category | flops | bytes accessed | tf_op | source)
XLA Modules:
  0.0 109.8 jit_solution(7651179458440075659)
XLA Ops:
  0.6 0.7 pad_maximum_fusion
  1.4 0.6 reshape.15.shard_ref
  2.0 96.8 %layer.1 = (bf16[2,24,48,512]{3,2,1,0:T(8,128)(2,1)}, bf16[2,24,48,512]{3,2,1,0:T(8,128)(2,1)}, bf16[2,2,3,48,512]{4,3,2,1,0:T(8,128)(2,1)}, bf16[2,2,12,16,512]...) custom-call(bf16[2,24,48,512]{3,2,1,0:T(8,128)(2,1)} %lat_ref.1, ...), custom_call_target="tpu_custom_call" | custom-call | tf_op jit(solution)/shard_map/layer/pallas_call | solution.py:493
  98.8 0.0 copy-start
  98.8 1.7 %copy-done = bf16[2,24,48,512]{3,2,1,0:T(8,128)(2,1)S(1)} copy-done((bf16[2,24,48,512]{3,2,1,0:T(8,128)(2,1)S(1)}, bf16[2,24,48,512]{3,2,1,0:T(8,128)(2,1)}, u32[]{:S(2)}) %copy-start) | copy-done | bytes 2359320
  100.5 0.0 copy-start.1
  100.5 1.7 %copy-done.1 = bf16[2,24,48,512]{3,2,1,0:T(8,128)(2,1)S(1)} copy-done((bf16[2,24,48,512]{3,2,1,0:T(8,128)(2,1)S(1)}, bf16[2,24,48,512]{3,2,1,0:T(8,128)(2,1)}, u32[]{:S(2)}) %copy-start.1) | copy-done | bytes 2359320
  102.1 0.0 copy-start.2
  102.1 1.1 %copy-done.2 = bf16[2,2,12,16,512]{4,3,2,1,0:T(8,128)(2,1)S(1)} copy-done((bf16[2,2,12,16,512]{4,3,2,1,0:T(8,128)(2,1)S(1)}, bf16[2,2,12,16,512]{4,3,2,1,0:T(8,128)(2,1)}, u32[]{:S(2)}) %copy-start.2) | copy-done | bytes 786456
  103.3 0.0 copy-start.3
  103.3 1.1 copy-done.3
  104.3 0.0 copy-start.4
  104.3 0.9 copy-done.4
  105.2 0.5 merge.1
  105.7 1.4 %copy.19 = bf16[2,24,48,512]{3,2,1,0:T(8,128)(2,1)} copy(bf16[2,24,48,512]{3,2,1,0:T(8,128)(2,1)S(1)} %get-tuple-element.26) | data formatting | bytes 4718592
  107.2 0.0 copy-start.5
  107.2 0.0 copy-start.6
  107.2 1.4 %copy.20 = bf16[2,24,48,512]{3,2,1,0:T(8,128)(2,1)} copy(bf16[2,24,48,512]{3,2,1,0:T(8,128)(2,1)S(1)} %get-tuple-element.27) | data formatting | bytes 4718592
  108.6 0.0 copy-done.5
  108.6 0.6 copy.21
  109.2 0.0 copy-done.6
  109.2 0.6 copy.22
  (2 shorter events, 0.0 us)
Async XLA Ops:
  98.8 1.7 %copy-start = (bf16[2,24,48,512]{3,2,1,0:T(8,128)(2,1)S(1)}, bf16[2,24,48,512]{3,2,1,0:T(8,128)(2,1)}, u32[]{:S(2)}) copy-start(bf16[2,24,48,512]{3,2,1,0:T(8,128)(2,1)} %get-tuple-element.13.out_in) | copy-start | bytes 7077892
  100.5 1.7 %copy-start.1 = (bf16[2,24,48,512]{3,2,1,0:T(8,128)(2,1)S(1)}, bf16[2,24,48,512]{3,2,1,0:T(8,128)(2,1)}, u32[]{:S(2)}) copy-start(bf16[2,24,48,512]{3,2,1,0:T(8,128)(2,1)} %get-tuple-element.14.grad_in) | copy-start | bytes 7077892
  102.1 1.1 %copy-start.2 = (bf16[2,2,12,16,512]{4,3,2,1,0:T(8,128)(2,1)S(1)}, bf16[2,2,12,16,512]{4,3,2,1,0:T(8,128)(2,1)}, u32[]{:S(2)}) copy-start(bf16[2,2,12,16,512]{4,3,2,1,0:T(8,128)(2,1)} %get-tuple-element.16.hc_ref) | copy-start | bytes 2359300
  103.3 1.1 copy-start.3
  104.3 0.9 copy-start.4
  107.2 1.4 %copy-start.5 = (f32[4,1536]{1,0:T(4,128)S(1)}, f32[4,1536]{1,0:T(4,128)}, u32[]{:S(2)}) copy-start(f32[4,1536]{1,0:T(4,128)} %get-tuple-element.28) | copy-start | bytes 73732
  107.2 2.0 %copy-start.6 = (f32[4,512]{1,0:T(4,128)S(1)}, f32[4,512]{1,0:T(4,128)}, u32[]{:S(2)}) copy-start(f32[4,512]{1,0:T(4,128)} %get-tuple-element.29) | copy-start | bytes 24580

commit v2 on v1

v2 whole, which is shorter than its diff:
```python
import functools
import math

import jax
import jax.numpy as jnp
from jax import lax
from jax.experimental import pallas as pl
from jax.experimental.pallas import tpu as pltpu
from jax.sharding import PartitionSpec as P

C = 512
HD = 64
WIN_LAT = 6
WIN_LON = 12
LEVELS = 2
PIECES = LEVELS * WIN_LAT
TOK = PIECES * WIN_LON
SLABS = 4
ACROSS = 4
WINDOWS = SLABS * ACROSS
TOKENS = WINDOWS * TOK
SLAB = ACROSS * TOK
HALF_ROWS = 3
HALF_COLS = 6
ROWS = 24
COLS = 48
TILES = ROWS // 2
HALF = 2 * C
BF = jnp.bfloat16
F32 = jnp.float32


def nn(a, b):
    return lax.dot_general(a, b, (((1,), (0,)), ((), ())), preferred_element_type=F32)


def nt(a, b):
    return lax.dot_general(a, b, (((1,), (1,)), ((), ())), preferred_element_type=F32)


def tn(a, b):
    return lax.dot_general(a, b, (((0,), (0,)), ((), ())), preferred_element_type=F32)


MESH = pl.DeviceIdType.MESH
GROUP = [(a, b, c) for a in range(2) for b in range(2) for c in range(2)][1:]


EDGE_STEP, ROWS_STEP = 2, 3


def first_token(slab, across):
    if isinstance(slab, int) and slab == SLABS - 1:
        return SLAB * ROWS_STEP + TOK * across
    if across == ACROSS - 1:
        return pl.multiple_of(SLAB * EDGE_STEP + TOK * (slab + 1), 16)
    return pl.multiple_of(TOK * (3 * slab + across), 16)


class Place:
    def __init__(self):
        self.lat, self.lon = lax.axis_index("lat"), lax.axis_index("lon")
        self.x_hi, self.y = self.lat // 4, self.lat % 4
        self.z, self.x_lo, self.core = self.lon // 4, (self.lon // 2) % 2, self.lon % 2

    def mate(self, flips):
        a, b, c = (v + f - 2 * v * f for v, f in zip((self.x_hi, self.x_lo, self.core), flips))
        return (a * 4 + self.y, self.z * 4 + b * 2 + c)

    def along(self, axis, step):
        if axis == "y":
            return (self.x_hi * 4 + (self.y + step) % 4, self.lon)
        return (self.lat, (self.z + step) % 4 * 4 + self.lon % 4)

    def shifted(self, rows, cols):
        return ((self.lat + rows + 8) % 8, (self.lon + cols + 16) % 16)


def greet(senders):
    barrier = pltpu.get_barrier_semaphore()
    for device in senders:
        pl.semaphore_signal(barrier, inc=1, device_id=device, device_id_type=MESH)
    pl.semaphore_wait(barrier, len(senders))


def remote(src, dst, sems, slot, device):
    return pltpu.make_async_remote_copy(
        src_ref=src, dst_ref=dst, send_sem=sems.at[0, slot], recv_sem=sems.at[1, slot],
        device_id=device, device_id_type=MESH)


def partners(place):
    return ([place.mate(f) for f in GROUP]
            + [place.along("y", s) for s in (1, 2, 3)] + [place.along("z", s) for s in (1, 2, 3)])


def fused_kernel(
    factor,
    lat_ref, cot_ref, qkv_shard, out_shard,
    out_ref, grad_ref, back_rows, back_cols, back_corner, sums_ref,
    grid, cols_in, corner_in, strip, corner_strip,
    shard_ref, shard_in, loose, weights,
    rows, window, results, inv_w, normed, ctx, gctx, qkv,
    lhs_t, gp, bias, bias_tail,
    cols_out,
    terms, from_mate, total, sent, from_near, from_far, relay, total2, sent2, from_second, sent3, from_group,
    grid_sems, halo_sems, group_sems, axis_sems, mate_sems, out_sems, back_sems, sum_sems, final_sems,
):
    place = Place()
    loads = [pltpu.make_async_copy(ref, grid.at[i, :, :ROWS], grid_sems.at[i]) for i, ref in enumerate((lat_ref, cot_ref))]
    for load in loads:
        load.start()
    near = [place.shifted(1, 0), place.shifted(0, 1), place.shifted(1, 1),
            place.shifted(-1, 0), place.shifted(0, -1), place.shifted(-1, -1)]
    barrier = pltpu.get_barrier_semaphore()
    for device in partners(place) + near:
        pl.semaphore_signal(barrier, inc=1, device_id=device, device_id_type=MESH)
    down, right, across_down, up, left, across_up = near

    def both(stage):
        for core in range(2):
            pl.when(place.core == core)(functools.partial(stage, core))

    for core in range(2):
        for block in range(4):
            for lane_tile in range(2):
                start = HALF * core + 256 * block + 128 * lane_tile
                piece = qkv_shard[:, start : start + 128] if start < 3 * C else out_shard[:, start - 3 * C : start - 3 * C + 128]
                loose[core, lane_tile, pl.ds(block, 4, stride=4)] = piece.astype(F32)
        shard_ref[core] = jnp.concatenate([loose[core, 0, :16], loose[core, 1, :16]], 1).astype(BF)

    pl.semaphore_wait(barrier, len(partners(place)) + len(near))

    here = (place.x_hi, place.x_lo, place.core)
    group = []
    for slot, flips in enumerate(GROUP):
        copy = remote(shard_ref.at[place.core if flips[2] == 0 else 1 - place.core],
                      shard_in.at[here], group_sems, slot, place.mate(flips))
        copy.start()
        group.append(copy)
    shard_in[here] = shard_ref[place.core]

    last = lax.axis_index("lat") == lax.axis_size("lat") - 1
    key = lax.broadcasted_iota(jnp.int32, (TOK, 128), 0)
    query = lax.broadcasted_iota(jnp.int32, (TOK, 128), 1)

    def flag(token):
        row = token // WIN_LON
        return jnp.where(row >= WIN_LAT, row - WIN_LAT, row) >= HALF_ROWS

    seam = jnp.where(last, -1e30, 0.0).astype(F32)
    bias[0] = jnp.zeros((TOK, 128), F32)
    bias_tail[0] = jnp.zeros((TOK, 128), F32)
    bias[1] = jnp.where(flag(key) != flag(query), seam, 0.0)
    bias_tail[1] = jnp.where(flag(key), 0.0, seam)

    for which in range(2):
        loads[which].wait()
        for level in range(LEVELS):
            def columns(row):
                return grid[which, level, row, :16].astype(F32)[:8]
            for tile in range(TILES - 1):
                first = HALF_ROWS + 2 * tile
                strip[which, level, tile] = jnp.concatenate(
                    [columns(first), columns(min(first + 1, ROWS - 1))], 0).astype(BF)
            corner_strip[which, level, 0] = jnp.concatenate([columns(0), columns(0)], 0).astype(BF)
            corner_strip[which, level, 1] = jnp.concatenate([columns(1), columns(2)], 0).astype(BF)
    halo_cols, halo_rows = [], []
    for which in range(2):
        halo_cols.append(remote(strip.at[which], cols_in.at[which, :, : TILES - 1], halo_sems, which, left))
        halo_rows.append(remote(corner_strip.at[which], corner_in.at[which], halo_sems, 2 + which, across_up))
        for level in range(LEVELS):
            halo_rows.append(remote(grid.at[which, level, :HALF_ROWS], grid.at[which, level, ROWS:], halo_sems,
                                    4 + 2 * which + level, up))

    for copy in group:
        copy.wait()
    for x_hi in range(2):
        for b in range(2):
            for c in range(2):
                for lane_tile in range(2):
                    line = 16 * (2 * b + c)
                    loose[x_hi, lane_tile, line : line + 16] = (
                        shard_in[x_hi, b, c][:, 128 * lane_tile : 128 * lane_tile + 128].astype(F32))
    def load_window(slab, across):
        start = HALF_COLS + WIN_LON * across
        low_col, high_col = start // 16 * 16, min(-(-(start + WIN_LON) // 16) * 16, COLS)
        for which in range(2):
            for level in range(LEVELS):
                for row in range(WIN_LAT):
                    piece = level * WIN_LAT + row
                    rows[which, piece, low_col:high_col] = (
                        grid[which, level, slab * WIN_LAT + row + HALF_ROWS, low_col:high_col].astype(F32))
                    if across == ACROSS - 1:
                        half = row % 2
                        rows[which, piece, COLS:] = (
                            cols_in[which, level, 3 * slab + row // 2].astype(F32)[8 * half : 8 * half + 8])
                    window[which, WIN_LON * piece : WIN_LON * (piece + 1)] = rows[which, piece, start : start + WIN_LON]
        part = pl.ds(first_token(slab, across), TOK)
        widened = window[0]
        centred = widened - jnp.mean(widened, -1, keepdims=True)
        inv = lax.rsqrt(jnp.mean(centred * centred, -1, keepdims=True) + 1e-05)
        results[0, part] = widened.astype(BF)
        inv_w[part] = inv
        normed[part] = (centred * inv).astype(BF)
        gp[part, 3 * C :] = window[1].astype(BF)

    def small_copies(core):
        block = weights.at[:, place.y, place.z, :, HALF * core : HALF * (core + 1)]
        return [remote(block, block, axis_sems, step - 1, place.along("z" if core == 0 else "y", step)) for step in (1, 2, 3)]

    def ring_block(core, step, x_hi=slice(None)):
        half = slice(HALF * core, HALF * (core + 1))
        if core == 0:
            return weights.at[x_hi, (place.y + step) % 4, :, :, half]
        return weights.at[x_hi, :, (place.z + step) % 4, :, half]

    def ring_copies(core):
        axis = "y" if core == 0 else "z"
        ahead, behind = place.along(axis, 1), place.along(axis, 3)
        piece = [ring_block(core, 0, 0), ring_block(core, 0, 1)]
        far, near = ring_block(core, 3, 0), ring_block(core, 1, 1)
        return ([remote(piece[i], piece[i], axis_sems, 3 + i, ahead) for i in (0, 1)],
                [remote(piece[i], piece[i], axis_sems, 5 + i, behind) for i in (1, 0)],
                [remote(far, far, axis_sems, 7, ahead), remote(near, near, axis_sems, 8, behind)])

    def mate_copies(core):
        other = place.mate((0, 0, 1))
        return [remote(ring_block(core, step), ring_block(core, step), mate_sems, slot, other)
                for slot, step in enumerate((0, 3, 1, 2))]

    def spread_shards(core):
        for x_hi in range(2):
            for block in range(4):
                for lane_tile in range(2):
                    start = HALF * core + 256 * block + 128 * lane_tile
                    weights[x_hi, place.y, place.z, :, start : start + 128] = (
                        loose[x_hi, lane_tile, pl.ds(block, 16, stride=4)].astype(BF))
        for copy in small_copies(core):
            copy.start()

    def ring_start(core):
        for copy in small_copies(core):
            copy.wait()
        ahead, behind, _ = ring_copies(core)
        for one, other in zip(ahead, behind):
            one.start()
            other.start()
        mate_copies(core)[0].start()

    def ring_relay(core):
        ahead, behind, far = ring_copies(core)
        mates = mate_copies(core)
        ahead[0].wait()
        far[0].start()
        behind[0].wait()
        far[1].start()
        ahead[1].wait()
        behind[1].wait()
        mates[1].start()
        mates[2].start()

    def ring_end(core):
        for copy in ring_copies(core)[2]:
            copy.wait()
        mate_copies(core)[3].start()

    def mates_end(core):
        for copy in mate_copies(core):
            copy.wait()

    @pl.loop(0, SLABS - 1)
    def _(slab):
        for when, stage in enumerate((spread_shards, ring_start, ring_relay)):
            for core in range(2):
                pl.when((slab == when) & (place.core == core))(functools.partial(stage, core))
        for across in range(ACROSS - 1):
            load_window(slab, across)

    both(ring_end)
    for copy in halo_cols + halo_rows:
        copy.start()
    both(mates_end)
    w_ref = weights.reshape(C, 4 * C)

    lane = lax.broadcasted_iota(jnp.int32, (1, 128), 1)
    low = (lane < HD).astype(F32).astype(BF)
    high = (lane >= HD).astype(F32).astype(BF)
    low_lanes = lax.broadcasted_iota(jnp.int32, (128, 128), 1) < HD
    low_lanes16 = lax.broadcasted_iota(jnp.int32, (16, 128), 1) < HD

    def spread(tail):
        zero = jnp.zeros((16, 128), BF)
        lines = []
        for head in range(8):
            pair = head // 2
            mine = tail[:, 128 * pair : 128 * (pair + 1)] * (low if head % 2 == 0 else high)
            lines.append(jnp.concatenate([mine if p == pair else zero for p in range(4)], 1))
        return jnp.concatenate(lines, 0)

    def gather(full, pair):
        cols = slice(128 * pair, 128 * (pair + 1))
        return jnp.where(low_lanes16, full[32 * pair : 32 * pair + 16, cols], full[32 * pair + 16 : 32 * pair + 32, cols])

    def softmax_both(scores, grad_att):
        top = jnp.max(scores, 0, keepdims=True)
        raised = jnp.exp(scores - top)
        att = raised * (1.0 / jnp.sum(raised, 0, keepdims=True))
        weighed = grad_att * att
        inner = jnp.sum(weighed, 0, keepdims=True)
        return att.astype(BF), (weighed - att * inner).astype(BF)

    def attend(base, seam_slab):
        offset = bias[seam_slab]
        offset = jnp.concatenate([offset, offset], 1)
        units = []
        for across in range(ACROSS):
            token = across * TOK
            main, tail, whole = slice(token, token + 128), slice(token + 128, token + TOK), slice(token, token + TOK)
            keys = qkv[whole, C : 2 * C]
            values = qkv[whole, 2 * C :]
            units.append((across, None, spread(qkv[tail, :C]), spread(gctx[tail]), keys, values))
            for pair in range(4):
                cols = slice(128 * pair, 128 * (pair + 1))
                q = qkv[main, cols]
                g = gctx[main, cols]
                q_both = jnp.concatenate([q * low, q * high], 0)
                g_both = jnp.concatenate([g * low, g * high], 0)
                units.append((across, pair, q_both, g_both, keys[:, cols], values[:, cols]))
        products = [(nt(k, q), nt(v, g)) for _, _, q, g, k, v in units]
        softened = []
        for unit, (scores, grad_att) in zip(units, products):
            softened.append(softmax_both(scores + (bias_tail[seam_slab] if unit[1] is None else offset), grad_att))
        made = [(tn(a, v), tn(s, k)) for (a, s), (_, _, q, g, k, v) in zip(softened, units)]
        made2 = [(nn(s, q), nn(a, g)) for (a, s), (_, _, q, g, k, v) in zip(softened, units)]
        for unit, (context, grad_q), (grad_k, grad_v) in zip(units, made, made2):
            across, pair = unit[:2]
            if pair is None:
                ctx_tail, gq_tail, gk_tail, gv_tail = context, grad_q, grad_k, grad_v
                continue
            token = across * TOK
            cols = slice(128 * pair, 128 * (pair + 1))
            g_main = pl.ds(pl.multiple_of(base + token, 16), 128)
            g_tail = pl.ds(pl.multiple_of(base + token + 128, 16), 16)
            g_whole = pl.ds(pl.multiple_of(base + token, 16), TOK)
            ctx[g_main, cols] = jnp.where(low_lanes, context[:128], context[128:]).astype(BF)
            ctx[g_tail, cols] = gather(ctx_tail, pair).astype(BF)
            gp[g_main, cols] = (jnp.where(low_lanes, grad_q[:128], grad_q[128:]) * HD ** -0.5).astype(BF)
            gp[g_tail, cols] = (gather(gq_tail, pair) * HD ** -0.5).astype(BF)
            gp[g_whole, C + 128 * pair : C + 128 * (pair + 1)] = (grad_k + gk_tail[:, cols]).astype(BF)
            gp[g_whole, 2 * C + 128 * pair : 2 * C + 128 * (pair + 1)] = (grad_v + gv_tail[:, cols]).astype(BF)

    def results_to_rows(slab, across):
        part = pl.ds(first_token(slab, across), TOK)
        start = HALF_COLS + WIN_LON * across
        for which in range(2):
            window[which] = results[which, part].astype(F32)
            for piece in range(PIECES):
                rows[which, piece, start : start + WIN_LON] = window[which, WIN_LON * piece : WIN_LON * (piece + 1)]

    def rows_to_strip(slab):
        for which in range(2):
            for level in range(LEVELS):
                for tile in range(3):
                    piece = level * WIN_LAT + 2 * tile
                    cols_out[which, level, 3 * slab + tile] = jnp.concatenate(
                        [rows[which, piece, COLS:], rows[which, piece + 1, COLS:]], 0).astype(BF)

    def store_slab(slab):
        for across in range(ACROSS):
            results_to_rows(slab, across)
        for which in range(2):
            for level in range(LEVELS):
                for row in range(WIN_LAT):
                    grid[which, level, slab * WIN_LAT + row + HALF_ROWS] = rows[which, level * WIN_LAT + row, :COLS].astype(BF)

    def out_copies(slab):
        first = slab * WIN_LAT + HALF_ROWS
        return [pltpu.make_async_copy(grid.at[which, :, pl.ds(first, WIN_LAT)], target.at[:, pl.ds(first, WIN_LAT)], out_sems.at[slab, which])
                for which, target in enumerate((out_ref, grad_ref))]

    def out_copies_last():
        return [pltpu.make_async_copy(grid.at[which, :, ROWS - HALF_ROWS : ROWS], target.at[:, ROWS - HALF_ROWS :],
                                      out_sems.at[SLABS - 1, which])
                for which, target in enumerate((out_ref, grad_ref))]

    def back_copies(slab):
        return [remote(cols_out.at[which, :, pl.ds(3 * slab, 3)], back_cols.at[which, :, pl.ds(3 * slab, 3)], back_sems,
                       2 * slab + which, right) for which in range(2)]

    def back_copies_last():
        copies = []
        for which in range(2):
            copies.append(remote(grid.at[which, :, ROWS:], back_rows.at[which], back_sems, 8 + which, down))
            copies.append(remote(cols_out.at[which, :, TILES - 2 :], back_corner.at[which], back_sems, 10 + which, across_down))
        return copies

    def finish(unit):
        part = pl.ds(pl.multiple_of(unit * SLAB, 64), SLAB)
        results[0, part] = (results[0, part].astype(F32) + nn(ctx[part], w_ref[:, 3 * C :])).astype(BF)
        grad_normed = nt(gp[part, : 3 * C], w_ref[:, : 3 * C])
        standard = normed[part].astype(F32)
        first_mean = jnp.mean(grad_normed, -1, keepdims=True)
        second_mean = jnp.mean(grad_normed * standard, -1, keepdims=True)
        results[1, part] = (inv_w[part] * (grad_normed - first_mean - standard * second_mean)
                            + gp[part, 3 * C :].astype(F32)).astype(BF)

    @pl.loop(0, SLABS)
    def _(step):
        base = pl.multiple_of(step * SLAB, 64)
        part = pl.ds(base, SLAB)

        @pl.when(step == 2)
        def _():
            for copy in halo_cols:
                copy.wait()

        @pl.when(step == EDGE_STEP)
        def _():
            @pl.loop(0, SLABS - 1)
            def _(slab):
                load_window(slab, ACROSS - 1)

        @pl.when(step == ROWS_STEP)
        def _():
            for copy in halo_rows:
                copy.wait()
            for which in range(2):
                for level in range(LEVELS):
                    cols_in[which, level, TILES - 2] = jnp.concatenate(
                        [cols_in[which, level, TILES - 2].astype(F32)[:8], corner_in[which, level, 0].astype(F32)[8:]], 0).astype(BF)
                    cols_in[which, level, TILES - 1] = corner_in[which, level, 1]
            for across in range(ACROSS):
                load_window(SLABS - 1, across)

        block = normed[part]
        for third in range(3):
            cols = slice(C * third, C * (third + 1))
            projected = nn(block, w_ref[:, cols]).astype(BF)
            qkv[:, cols] = projected * BF(HD ** -0.5) if third == 0 else projected
        gctx[...] = nt(gp[part, 3 * C :], w_ref[:, 3 * C :]).astype(BF)
        attend(base, step // 3 if ROWS_STEP == 3 else step // 2 * (1 - step // 3))
        @pl.when(step >= 2)
        def _():
            finish(step)

        @pl.when(step == EDGE_STEP)
        def _():
            @pl.loop(0, SLABS - 1)
            def _(slab):
                results_to_rows(slab, ACROSS - 1)
                rows_to_strip(slab)
                for copy in back_copies(slab):
                    copy.start()

        @pl.when(step == ROWS_STEP)
        def _():
            store_slab(SLABS - 1)
            rows_to_strip(SLABS - 1)
            for copy in back_copies_last() + back_copies(SLABS - 1) + out_copies_last():
                copy.start()

        @pl.when(step % 2 == 1)
        def _():
            two = pl.ds(pl.multiple_of(step // 2 * (2 * SLAB), 128), 2 * SLAB)
            lhs_t[0, :, two] = normed[two].T
            lhs_t[1, :, two] = ctx[two].T

    other = place.mate((0, 0, 1))

    def columns_of(half, part):
        return (half * 2 + part) % 4

    def product(block):
        return nn(lhs_t[block // 3], gp[:, pl.ds(pl.multiple_of(block * C, 128), C)])

    def mate_copy(part):
        return remote(terms.at[part], from_mate.at[part], sum_sems, part, other)

    @pl.loop(0, 2)
    def _(part):
        terms[part] = product(columns_of(1 - place.core, part)).astype(BF).reshape(2, 4, 4, 16, C)
        mate_copy(part).start()

    @pl.loop(0, 2)
    def _(part):
        mate_copy(part).wait()
        added = product(columns_of(place.core, part)) + from_mate[part].reshape(C, C).astype(F32)
        total[part] = added.reshape(2, 4, 4, 16, C)
        sent[part] = added.astype(BF).reshape(2, 4, 4, 16, C)

    def sum_block(core, ref, step, x_hi):
        if core == 0:
            return ref.at[:, x_hi, (place.y + step) % 4]
        return ref.at[:, x_hi, :, (place.z + step) % 4]

    def sum_copies(core):
        axis = "y" if core == 0 else "z"
        ahead, behind = place.along(axis, 1), place.along(axis, 3)
        far = [remote(sum_block(core, sent, 2, 0), from_far.at[0], sum_sems, 2, ahead),
               remote(sum_block(core, sent, 2, 1), from_far.at[1], sum_sems, 3, behind)]
        plain = [remote(sum_block(core, sent, 1, 1), from_near.at[0, 1], sum_sems, 4, ahead),
                 remote(sum_block(core, sent, 3, 0), from_near.at[1, 0], sum_sems, 5, behind)]
        summed = [remote(relay.at[0], from_near.at[0, 0], sum_sems, 6, ahead),
                  remote(relay.at[1], from_near.at[1, 1], sum_sems, 7, behind)]
        return far, plain, summed

    def second_copies(core):
        mine = place.z if core == 0 else place.y
        return [remote(sent2.at[:, :, (mine + step) % 4], from_second.at[step - 1], sum_sems, 8 + step - 1,
                       place.along("z" if core == 0 else "y", step)) for step in (1, 2, 3)]

    def sum_start(core):
        far, plain, _ = sum_copies(core)
        for copy in far + plain:
            copy.start()

    def sum_relay(core):
        far, _, summed = sum_copies(core)
        for way, (step, x_hi) in enumerate(((1, 0), (3, 1))):
            far[way].wait()
            relay[way] = (sum_block(core, total, step, x_hi)[...] + from_far[way].astype(F32)).astype(BF)
            summed[way].start()

    def sum_second(core):
        _, plain, summed = sum_copies(core)
        for copy in plain + summed:
            copy.wait()
        for x_hi in range(2):
            added = (sum_block(core, total, 0, x_hi)[...] + from_near[0, x_hi].astype(F32)
                     + from_near[1, x_hi].astype(F32))
            total2[x_hi] = added
            sent2[x_hi] = added.astype(BF)
        for copy in second_copies(core):
            copy.start()

    def sum_third(core):
        for copy in second_copies(core):
            copy.wait()
        added = total2[:, :, place.z if core == 0 else place.y]
        for step in range(3):
            added = added + from_second[step].astype(F32)
        sent3[...] = added.astype(BF)

    @pl.loop(0, 2)
    def _(unit):
        for when, stage in enumerate((sum_start, sum_relay)):
            for core in range(2):
                pl.when((unit == when) & (place.core == core))(functools.partial(stage, core))
        finish(unit)

    both(sum_second)

    @pl.loop(0, SLABS - 1)
    def _(slab):
        store_slab(slab)
        for copy in out_copies(slab):
            copy.start()

    both(sum_third)
    copies = []
    for slot, flips in enumerate(GROUP):
        target = place.x_hi if flips[0] == 0 else 1 - place.x_hi
        copies.append(remote(sent3.at[target], from_group.at[here], final_sems, slot, place.mate(flips)))
    for copy in copies:
        copy.start()
    from_group[here] = sent3[place.x_hi]
    for copy in copies:
        copy.wait()
    position = place.x_lo * 2 + place.core
    for block in range(4):
        added = from_group[0, 0, block // 2, block % 2].astype(F32)
        for a, b in ((0, 1), (1, 0), (1, 1)):
            added = added + from_group[a, b, block // 2, block % 2].astype(F32)
        picked = added[:4]
        for i in range(1, 4):
            picked = jnp.where(position == i, added[4 * i : 4 * i + 4], picked)
        sums_ref[:, C * block : C * (block + 1)] = picked * factor
    for slab in range(SLABS):
        for copy in back_copies(slab):
            copy.wait()
    for slab in range(SLABS - 1):
        for copy in out_copies(slab):
            copy.wait()
    for copy in out_copies_last() + back_copies_last():
        copy.wait()


def fused(latent, cotangent, qkv_weight, out_weight, factor):
    anywhere = pl.BlockSpec(memory_space=pltpu.HBM)
    whole = pl.BlockSpec(memory_space=pltpu.VMEM)
    grid_shape = jax.ShapeDtypeStruct((LEVELS, ROWS, COLS, C), BF)
    dma = pltpu.SemaphoreType.DMA
    return pl.pallas_call(
        functools.partial(fused_kernel, factor),
        out_shape=(
            grid_shape,
            grid_shape,
            jax.ShapeDtypeStruct((2, LEVELS, HALF_ROWS, COLS, C), BF),
            jax.ShapeDtypeStruct((2, LEVELS, TILES, 16, C), BF),
            jax.ShapeDtypeStruct((2, LEVELS, 2, 16, C), BF),
            jax.ShapeDtypeStruct((4, 4 * C), F32),
        ),
        in_specs=[anywhere, anywhere, whole, whole],
        out_specs=(anywhere,) * 5 + (whole,),
        scratch_shapes=[
            pltpu.VMEM((2, LEVELS, ROWS + HALF_ROWS, COLS, C), BF),
            pltpu.VMEM((2, LEVELS, TILES, 16, C), BF),
            pltpu.VMEM((2, LEVELS, 2, 16, C), BF),
            pltpu.VMEM((2, LEVELS, TILES - 1, 16, C), BF),
            pltpu.VMEM((2, LEVELS, 2, 16, C), BF),
            pltpu.VMEM((2, 16, 256), BF),
            pltpu.VMEM((2, 2, 2, 16, 256), BF),
            pltpu.VMEM((2, 2, 64, 128), F32),
            pltpu.VMEM((2, 4, 4, 16, 4 * C), BF),
            pltpu.VMEM((2, PIECES, COLS + 8, C), F32),
            pltpu.VMEM((2, TOK, C), F32),
            pltpu.VMEM((2, TOKENS, C), BF),
            pltpu.VMEM((TOKENS, 1), F32),
            pltpu.VMEM((TOKENS, C), BF),
            pltpu.VMEM((TOKENS, C), BF),
            pltpu.VMEM((SLAB, C), BF),
            pltpu.VMEM((SLAB, 3 * C), BF),
            pltpu.VMEM((2, C, TOKENS), BF),
            pltpu.VMEM((TOKENS, 4 * C), BF),
            pltpu.VMEM((2, TOK, 128), F32),
            pltpu.VMEM((2, TOK, 128), F32),
            pltpu.VMEM((2, LEVELS, TILES, 16, C), BF),
            pltpu.VMEM((2, 2, 4, 4, 16, C), BF),
            pltpu.VMEM((2, 2, 4, 4, 16, C), BF),
            pltpu.VMEM((2, 2, 4, 4, 16, C), F32),
            pltpu.VMEM((2, 2, 4, 4, 16, C), BF),
            pltpu.VMEM((2, 2, 2, 4, 16, C), BF),
            pltpu.VMEM((2, 2, 4, 16, C), BF),
            pltpu.VMEM((2, 2, 4, 16, C), BF),
            pltpu.VMEM((2, 2, 4, 16, C), F32),
            pltpu.VMEM((2, 2, 4, 16, C), BF),
            pltpu.VMEM((3, 2, 2, 16, C), BF),
            pltpu.VMEM((2, 2, 16, C), BF),
            pltpu.VMEM((2, 2, 2, 2, 16, C), BF),
            dma((2,)),
            dma((2, 8)),
            dma((2, 7)),
            dma((2, 9)),
            dma((2, 4)),
            dma((SLABS, 2)),
            dma((2, 12)),
            dma((2, 11)),
            dma((2, 7)),
        ],
        compiler_params=pltpu.CompilerParams(
            collective_id=0, has_side_effects=True, vmem_limit_bytes=62 * 2**20),
        name="layer",
    )(latent, cotangent, qkv_weight, out_weight)


def merge_kernel(
    out_in, grad_in, hr_hbm, hc_hbm, hd_hbm, sums_ref, out_ref, grad_ref, qkv_ref, o_ref,
    grid, hr_ref, hc_ref, hd_ref, load_sems, store_sems,
):
    parts = [(which, level) for which in range(2) for level in range(LEVELS)]
    loads = []
    for which, level in parts:
        loads.append([pltpu.make_async_copy(src.at[which, level], dst.at[which, level], load_sems.at[which, level, i])
                      for i, (src, dst) in enumerate(((hc_hbm, hc_ref), (hd_hbm, hd_ref), (hr_hbm, hr_ref)))])
        own = (out_in, grad_in)[which].at[level, HALF_ROWS:]
        loads[-1].append(pltpu.make_async_copy(own, grid.at[which, level, HALF_ROWS:], load_sems.at[which, level, 3]))
        for load in loads[-1]:
            load.start()
    qkv_ref[...] = sums_ref[:, : 3 * C]
    o_ref[...] = sums_ref[:, 3 * C :]
    column = lax.broadcasted_iota(jnp.int32, (16, C), 0)
    blank = jnp.zeros((8, C), F32)
    stores = []
    for (which, level), coming in zip(parts, loads):
        for load in coming:
            load.wait()
        for row in range(ROWS):
            line = (row - HALF_ROWS) % ROWS
            ref = hc_ref if row >= HALF_ROWS else hd_ref
            tile = line // 2 if row >= HALF_ROWS else line // 2 - (TILES - 2)
            half = line % 2
            halo = jnp.concatenate([ref[which, level, tile].astype(F32)[8 * half : 8 * half + 8], blank], 0)
            own = grid[which, level, row, :16] if row >= HALF_ROWS else hr_ref[which, level, row, :16]
            grid[which, level, row, :16] = jnp.where(column < HALF_COLS, halo, own.astype(F32)).astype(BF)
            if row < HALF_ROWS:
                grid[which, level, row, 16:] = hr_ref[which, level, row, 16:]
        stores.append(pltpu.make_async_copy(grid.at[which, level], (out_ref, grad_ref)[which].at[level],
                                            store_sems.at[which, level]))
        stores[-1].start()
    for store in stores:
        store.wait()


def merge(out, grad, row_strip, col_strip, corner, sums):
    anywhere = pl.BlockSpec(memory_space=pltpu.HBM)
    whole = pl.BlockSpec(memory_space=pltpu.VMEM)
    grid_shape = jax.ShapeDtypeStruct((LEVELS, ROWS, COLS, C), BF)
    return pl.pallas_call(
        merge_kernel,
        out_shape=(grid_shape, grid_shape, jax.ShapeDtypeStruct((4, 3 * C), F32), jax.ShapeDtypeStruct((4, C), F32)),
        in_specs=[anywhere] * 5 + [whole],
        out_specs=(anywhere, anywhere, whole, whole),
        scratch_shapes=[
            pltpu.VMEM((2, LEVELS, ROWS, COLS, C), BF),
            pltpu.VMEM((2, LEVELS, HALF_ROWS, COLS, C), BF),
            pltpu.VMEM((2, LEVELS, TILES, 16, C), BF),
            pltpu.VMEM((2, LEVELS, 2, 16, C), BF),
            pltpu.SemaphoreType.DMA((2, LEVELS, 4)),
            pltpu.SemaphoreType.DMA((2, LEVELS)),
        ],
        compiler_params=pltpu.CompilerParams(vmem_limit_bytes=62 * 2**20),
        name="merge",
    )(out, grad, row_strip, col_strip, corner, sums)


def body(latent, cotangent, qkv_weight, out_weight):
    total_tokens = TOKENS * lax.axis_size("lat") * lax.axis_size("lon")
    done = fused(latent, cotangent, qkv_weight, out_weight, 1.0 / math.sqrt(total_tokens))
    return merge(*done)


def solution(mesh):
    grid = P(None, "lat", "lon", None)
    rows = P(("lat", "lon"), None)
    specs = (grid, grid, rows, rows)
    return jax.shard_map(body, mesh=mesh, in_specs=specs, out_specs=specs, check_vma=False)
```

time: 110 us -> 100 us (0.909)
  local copies, waits for them, and re-layouts: 11.1 us -> 0 us
  Pallas kernels: 97.3 us -> 99.2 us
    unnamed x18 -> x0, local copies, waits for them, and re-layouts: 10.4 us -> none
    pallas_call x1, Pallas kernels: 0.5 us -> 5.97 us  [merge(): pl.pallas_call(merge_kernel, out_shape=(grid_shape, grid_shape, jax.Shape...]
    pallas_call x1, Pallas kernels: 96.8 us -> 93.3 us  [fused(): pl.pallas_call(functools.partial(fused_kernel, factor), out_shape=(grid_s...]
where the time goes in v2:
time: 100 us
  Pallas kernels  99.2 us (99%)
    pallas_call x1, Pallas kernels, fused(): pl.pallas_call(functools.partial(fused_kernel, factor), out_shape=(grid_s...  93.3 us
    pallas_call x1, Pallas kernels, merge(): pl.pallas_call(merge_kernel, out_shape=(grid_shape, grid_shape, jax.Shape...  5.97 us

profile of v2, /device:TPU:1, one launch (start us, length us, event | category | flops | bytes accessed | tf_op | source)
XLA Modules:
  0.0 100.0 jit_solution(11927977887336574045)
XLA Ops:
  0.6 93.3 %layer.1 = (bf16[2,24,48,512]{3,2,1,0:T(8,128)(2,1)}, bf16[2,24,48,512]{3,2,1,0:T(8,128)(2,1)}, bf16[2,2,3,48,512]{4,3,2,1,0:T(8,128)(2,1)}, bf16[2,2,12,16,512]...) custom-call(bf16[2,24,48,512]{3,2,1,0:T(8,128)(2,1)} %lat_ref.1, ...), custom_call_target="tpu_custom_call" | custom-call | tf_op jit(solution)/shard_map/layer/pallas_call | solution.py:594
  93.9 6.0 %merge.1 = (bf16[2,24,48,512]{3,2,1,0:T(8,128)(2,1)}, bf16[2,24,48,512]{3,2,1,0:T(8,128)(2,1)}, f32[4,1536]{1,0:T(4,128)}, f32[4,512]{1,0:T(4,128)}) custom-call(bf16[2,24,48,512]{3,2,1,0:T(8,128)(2,1)} %get-tuple-element.10.out_in, bf16[2,24,48,512]{3,2,1,0:T(8,128)(2,1)} %get-tuple-element.11.grad_in, ...), custom_call_target="tpu_custom_call" | custom-call | tf_op jit(solution)/shard_map/merge/pallas_call | solution.py:699
